TPU v7x, 128 devices: a whole 4x4x4 slice. The times are simulated.
128 devices in a mesh: owner: 8 (over y, core), tile: 16 (over z, x).
Axes of the slice: x: 4, y: 4, z: 4, core: 2. Of those that a mesh axis runs over, the one named last changes fastest.
Arguments:
- embeddings: bfloat16 [131072, 1024], P(('owner', 'tile')), may hold values from -40 to 40, as said below
- sorted_pos: int32 [131072], P(('owner', 'tile')), may hold values from 0 to 131071, as said below
- block_cluster: int32 [1024], P(('owner', 'tile')), may hold values from 0 to 63, as said below
- tile_list: int32 [8, 16, 2, 8320], P('owner', 'tile'), may hold values from -1 to 127, as said below
Outputs:
- max_sim: float32 [131072], P(('owner', 'tile'))
Inputs may be any that keep to these rules, and one draw needn't show every extreme that they name: Raw embeddings with row scales within a factor of ten. `sorted_pos`: A permutation; the rows of each device go to exactly 8 positions in each device's range of 1024 cluster-order positions. `block_cluster`: never falling; each cluster is a run of whole blocks inside one group of 128 blocks (the blocks held by one index of owner), and group g holds exactly the clusters g * 8 to (g + 1) * 8 - 1. `tile_list`: over the workers of one group, every pair rb >= cb of the group's blocks in one cluster is listed exactly once; unused entries are -1 in both places and follow a worker's used ones; workers' lists differ in length.
All inputs are finite; a program needn't handle non-finite values.
Results may differ from a plain program's by a relative error of at most 0.0005.
Values may be sent and summed in bfloat16 or wider, within the bound.
A program may use at most 192 MiB of HBM per device.

v0:
```python
import jax
import jax.numpy as jnp
from jax import lax
from jax.sharding import PartitionSpec as P

D = 1024
BLK = 128
ROW_DEV = 1024


def tile_batches(
    carry,
    query_blocks,
    query_clusters,
    query_base,
    column_blocks,
    column_clusters,
    column_base,
    row_list,
    col_list,
    lower,
    upper,
):
    span_size = 64
    final_entry = row_list.shape[0] - 1
    turn_count = (upper - lower + span_size - 1) // span_size
    lanes = jnp.arange(span_size, dtype=jnp.int32)
    inner = jnp.arange(BLK, dtype=jnp.int32)

    def advance(step, best):
        wanted = lower + step * span_size + lanes
        active = wanted < upper
        chosen = jnp.minimum(wanted, final_entry)
        row_ids = jnp.clip(row_list[chosen], 0, query_blocks.shape[0] - 1)
        col_ids = jnp.clip(col_list[chosen] - column_base, 0, column_blocks.shape[0] - 1)
        queries = query_blocks[row_ids]
        columns = column_blocks[col_ids]
        scores = jnp.einsum("tid,tjd->tij", queries, columns, preferred_element_type=jnp.float32)
        row_at = (query_base + row_ids)[:, None] * BLK + inner[None, :]
        col_at = (column_base + col_ids)[:, None] * BLK + inner[None, :]
        same = query_clusters[row_ids] == column_clusters[col_ids]
        counted = (active & same)[:, None, None] & (col_at[:, None, :] < row_at[:, :, None])
        highest = jnp.max(jnp.where(counted, scores, -1.0), axis=2)
        return best.at[row_ids].max(highest)

    return lax.fori_loop(0, turn_count, advance, carry)


def per_device(embeddings, sorted_pos, block_cluster, tile_list):
    owners = lax.axis_size("owner")
    workers = lax.axis_size("tile")
    devices_all = owners * workers
    pair_rows = ROW_DEV // devices_all
    blocks_here = ROW_DEV // BLK
    group_blocks = blocks_here * workers
    worker_index = lax.axis_index("tile")
    device_index = lax.axis_index("owner") * workers + worker_index
    values = embeddings.astype(jnp.float32)
    unit = (values * lax.rsqrt(jnp.sum(values * values, axis=1, keepdims=True) + 1e-06)).astype(
        jnp.bfloat16
    )
    ranked = jnp.argsort(sorted_pos)
    send_rows = unit[ranked].reshape(devices_all, pair_rows, D)
    send_slots = sorted_pos[ranked].reshape(devices_all, pair_rows)
    recv_rows, recv_slots = (
        lax.all_to_all(send_rows, ("owner", "tile"), split_axis=0, concat_axis=0, tiled=True),
        lax.all_to_all(send_slots, ("owner", "tile"), split_axis=0, concat_axis=0, tiled=True),
    )
    local_slots = recv_slots.reshape(ROW_DEV) - device_index * ROW_DEV
    ordered = (
        jnp.zeros((ROW_DEV, D), jnp.bfloat16).at[local_slots].set(recv_rows.reshape(ROW_DEV, D))
    )
    row_cluster = jnp.repeat(block_cluster, BLK)
    group_rows, group_cluster = (
        lax.all_gather(ordered, "tile", axis=0, tiled=True),
        lax.all_gather(row_cluster, "tile", axis=0, tiled=True),
    )
    row_list = tile_list[0, 0, 0]
    col_list = tile_list[0, 0, 1]
    entry_count = jnp.sum((row_list >= 0).astype(jnp.int32))
    group_tiles = group_rows.reshape(group_blocks, BLK, D)
    tile_clusters = group_cluster.reshape(group_blocks, BLK)[:, 0]
    start_best = jnp.full((group_blocks, BLK), -1.0, jnp.float32)
    partial_value = tile_batches(
        start_best,
        group_tiles,
        tile_clusters,
        0,
        group_tiles,
        tile_clusters,
        0,
        row_list,
        col_list,
        0,
        entry_count,
    )
    partial_parts = lax.all_to_all(
        partial_value.reshape(workers, ROW_DEV), "tile", split_axis=0, concat_axis=0, tiled=True
    )
    best_here = jnp.max(partial_parts, axis=0)
    answers = best_here[local_slots].reshape(devices_all, pair_rows)
    returned = lax.all_to_all(answers, ("owner", "tile"), split_axis=0, concat_axis=0, tiled=True)
    return jnp.zeros((ROW_DEV,), jnp.float32).at[ranked].set(returned.reshape(ROW_DEV))


def solution(mesh):
    placed = (
        P(("owner", "tile"), None),
        P(("owner", "tile")),
        P(("owner", "tile")),
        P("owner", "tile", None, None),
    )
    return jax.shard_map(
        per_device, mesh=mesh, in_specs=placed, out_specs=P(("owner", "tile")), check_vma=False
    )
```

profile of v0, /device:TPU:1, one launch (start us, length us, event | category | flops | bytes accessed | tf_op | source)
XLA Modules:
  0.0 764.7 jit_solution(2334584327203331218)
XLA Ops:
  6.5 0.0 copy-start
  6.5 0.0 copy-start.2
  6.5 5.2 sort.17
  11.7 0.6 broadcast_clamp_fusion.1
  12.3 5.7 gather_fusion.6
  18.1 0.7 all_to_all.21
  18.8 11.5 %all-to-all-start = ((s32[128,1,8]{2,1,0:T(1,128)}), s32[128,1,8]{2,1,0:T(1,128)S(1)}, u32[]{:S(2)}, u32[]{:S(2)}) async-start(s32[128,1,8]{2,1,0:T(1,128)} %bitcast.2), calls=%async_computation | async-start | bytes 131072 | tf_op jit(solution)/shard_map/all_to_all | solution.py:67
  30.3 0.0 copy-done.2
  30.3 0.5 fusion.8
  30.8 2.0 fusion.9
  32.8 5.4 gather_fusion.7
  38.1 1.9 all-to-all-done
  40.0 7.9 %all-to-all-start.1 = ((bf16[128,8,1024]{2,1,0:T(8,128)(2,1)}), bf16[128,8,1024]{2,1,0:T(8,128)(2,1)S(1)}, u32[]{:S(2)}, u32[]{:S(2)}) async-start(bf16[128,8,1024]{2,1,0:T(8,128)(2,1)} %bitcast.43), calls=%async_computation.1 | async-start | bytes 4194304 | tf_op jit(solution)/shard_map/all_to_all | solution.py:66
  47.9 0.0 copy-start.3
  47.9 0.0 all-gather.2.cloned.1.call-start
  48.0 0.2 subtract_reduce_fusion
  48.2 0.1 sub.27
  48.3 0.0 copy-start.4
  48.3 29.1 %all-to-all-done.1 = bf16[128,8,1024]{2,1,0:T(8,128)(2,1)S(1)} async-done(((bf16[128,8,1024]{2,1,0:T(8,128)(2,1)}), bf16[128,8,1024]{2,1,0:T(8,128)(2,1)S(1)}, u32[]{:S(2)}, u32[]{:S(2)}) %all-to-all-start.1) | async-done | bytes 2097184 | tf_op jit(solution)/shard_map/all_to_all | solution.py:66
  77.4 6.8 scatter_custom_fusion.1
  84.2 0.0 all-gather.2.cloned.1.call-update
  84.2 0.0 copy-done.3
  84.2 0.2 slice_reduce_fusion.1
  84.4 0.7 convert_reduce_fusion
  85.8 0.0 copy-done
  85.8 0.1 broadcast_bitcast_fusion
  85.8 18.9 %all_gather.6 = s32[16384]{0:T(1024)S(1)} all-gather(s32[1024]{0:T(1024)S(1)} %broadcast_bitcast_fusion), channel_id=1, replica_groups=mesh['owner'=8,'tile'=16] {'tile'}, dimensions={0}, use_global_device_ids=true | all-gather | bytes 69632 | tf_op jit(solution)/shard_map/all_gather | solution.py:76
  104.8 0.1 slice_reduce_fusion
  104.9 173.5 %all-gather.2.cloned.1.call-done = bf16[16384,1024]{1,0:T(8,128)(2,1)} async-done(((bf16[1024,1024]{1,0:T(8,128)(2,1)}), bf16[16384,1024]{1,0:T(8,128)(2,1)}) %all-gather.2.cloned.1.call-update) | async-done | bytes 33554448 | tf_op jit(solution)/shard_map/all_gather | solution.py:75
  278.4 0.6 broadcast_in_dim.15
  279.0 0.0 copy-done.4
  279.0 41.2 %while.12 = (s32[]{:T(128)}, f32[128,128]{1,0:T(8,128)}, s32[]{:T(128)}, s32[8320]{0:T(1024)S(1)}, s32[]{:T(128)}, /*index=5*/s32[128]{0:T(128)S(1)}, s32[8320]{...) while((s32[]{:T(128)}, f32[128,128]{1,0:T(8,128)}, s32[]{:T(128)}, ...), condition=%wide.region_7.8_spmd.clone.clone, body=%wide.region_4.7_spmd.clone.clone.sunk | while | flops 2151698688 | bytes 100945928 | solution.py:46
  279.0 0.8 gather_fusion
  279.8 0.8 gather_fusion.1
  280.6 0.1 iota_add_fusion.4
  280.7 0.8 gather_fusion.2
  281.5 0.8 gather_fusion.3
  282.3 0.6 compare_and_fusion.2
  282.9 11.1 %gather_fusion.4 = bf16[64,128,1024]{2,1,0:T(8,128)(2,1)} fusion(bf16[128,128,1024]{2,1,0:T(8,128)(2,1)} %get-tuple-element.212, s32[1024]{0:T(1024)S(1)} %pad_clamp_fusion.7), kind=kCustom, calls=%fused_computation.4.clone.clone.1 | custom fusion | bytes 33554688 | tf_op jit(solution)/shard_map/while/body/gather | solution.py:36
  294.0 10.9 %gather_fusion.5 = bf16[64,128,1024]{2,1,0:T(8,128)(2,1)} fusion(bf16[128,128,1024]{2,1,0:T(8,128)(2,1)} %get-tuple-element.212, s32[1024]{0:T(1024)S(1)} %pad_clamp_fusion.8), kind=kCustom, calls=%fused_computation.5.clone.clone.1 | custom fusion | bytes 33554688 | tf_op jit(solution)/shard_map/while/body/gather | solution.py:37
  304.8 12.9 %select_reduce_fusion.2 = f32[64,128]{1,0:T(8,128)S(1)} fusion(s32[64,128]{1,0:T(8,128)S(1)} %get-tuple-element.183, s32[64,128]{1,0:T(8,128)S(1)} %get-tuple-element.184, pred[64]{0:T(512)(128)(4,1)S(1)} %compare_and_fusion.2, bf16[64,128,1024]{2,1,0:T(8,128)(2,1)} %gather_fusion.4, bf16[64,128,1024]{2,1,0:T(8,128)(2,1)} %gather_fusion.5), kind=kOutput, calls=%fused_computation.14.clone.1 | convolution fusion | flops 2151669760 | bytes 33652800 | tf_op jit(solution)/shard_map/while/body/tid,tjd->tij/dot_general | solution.py:38
  317.8 2.4 scatter_fusion
  320.2 0.0 copy-start.1
  320.2 274.7 %all-to-all-start.2 = ((f32[16,1,1024]{2,1,0:T(1,128)}), f32[16,1,1024]{2,1,0:T(1,128)S(1)}, u32[]{:S(2)}, u32[]{:S(2)}) async-start(f32[16,1,1024]{2,1,0:T(1,128)} %bitcast.7), calls=%async_computation.2 | async-start | bytes 131072 | tf_op jit(solution)/shard_map/all_to_all | solution.py:97
  594.9 0.7 broadcast_clamp_fusion
  595.6 5.8 all-to-all-done.2
  601.5 0.1 reduce_max.18
  601.5 4.5 gather_fusion.8
  606.0 0.1 all_to_all.26
  606.1 145.3 %all_to_all.32 = f32[128,1,8]{2,1,0:T(1,128)S(1)} all-to-all(f32[128,1,8]{2,1,0:T(1,128)S(1)} %bitcast.45), channel_id=1, replica_groups=mesh['owner'=8,'tile'=16] {'owner','tile'}, dimensions={0} | all-to-all | bytes 8192 | tf_op jit(solution)/shard_map/all_to_all | solution.py:102
  751.4 0.5 broadcast.272
  751.9 0.8 reduce.14
  752.8 0.1 reshape.284
  752.9 5.0 scatter_custom_fusion.2
  757.9 0.0 copy-done.1
  (11 shorter events, 0.1 us)
Async XLA Ops:
  6.5 79.2 %copy-start = (s32[8]{0:T(128)S(1)}, s32[8]{0:T(128)}, u32[]{:S(2)}) copy-start(s32[8]{0:T(128)} %param.8) | copy-start | bytes 100
  6.5 23.7 %copy-start.2 = (bf16[1024,1024]{1,0:T(8,128)(2,1)S(1)}, bf16[1024,1024]{1,0:T(8,128)(2,1)}, u32[]{:S(2)}) copy-start(bf16[1024,1024]{1,0:T(8,128)(2,1)} %param.6) | copy-start | bytes 6291460
  18.8 21.3 %all-to-all-start = ((s32[128,1,8]{2,1,0:T(1,128)}), s32[128,1,8]{2,1,0:T(1,128)S(1)}, u32[]{:S(2)}, u32[]{:S(2)}) async-start(s32[128,1,8]{2,1,0:T(1,128)} %bitcast.2), calls=%async_computation | async-start | bytes 131072 | tf_op jit(solution)/shard_map/all_to_all | solution.py:67
  40.0 37.4 %all-to-all-start.1 = ((bf16[128,8,1024]{2,1,0:T(8,128)(2,1)}), bf16[128,8,1024]{2,1,0:T(8,128)(2,1)S(1)}, u32[]{:S(2)}, u32[]{:S(2)}) async-start(bf16[128,8,1024]{2,1,0:T(8,128)(2,1)} %bitcast.43), calls=%async_computation.1 | async-start | bytes 4194304 | tf_op jit(solution)/shard_map/all_to_all | solution.py:66
  47.9 36.3 %copy-start.3 = (s32[1,1,2,8320]{3,2,1,0:T(2,128)S(1)}, s32[1,1,2,8320]{3,2,1,0:T(2,128)}, u32[]{:S(2)}) copy-start(s32[1,1,2,8320]{3,2,1,0:T(2,128)} %param.9) | copy-start | bytes 199684
  47.9 230.5 %all-gather.2.cloned.1.call-start = ((), (), s32[]{:S(2)}) async-start(), calls=%async_computation.4 | async-start | bytes 35651584 | tf_op jit(solution)/shard_map/all_gather | solution.py:75
  48.3 230.7 %copy-start.4 = (s32[1024,1]{0,1:T(1,128)}, s32[1024,1]{0,1:T(1,128)S(1)}, u32[]{:S(2)}) copy-start(s32[1024,1]{0,1:T(1,128)S(1)} %compare_select_fusion.3) | copy-start | bytes 12292
  320.2 437.7 %copy-start.1 = (s32[8]{0:T(128)S(1)}, s32[8]{0:T(128)}, u32[]{:S(2)}) copy-start(s32[8]{0:T(128)} %param.8) | copy-start | bytes 100
  320.2 281.3 %all-to-all-start.2 = ((f32[16,1,1024]{2,1,0:T(1,128)}), f32[16,1,1024]{2,1,0:T(1,128)S(1)}, u32[]{:S(2)}, u32[]{:S(2)}) async-start(f32[16,1,1024]{2,1,0:T(1,128)} %bitcast.7), calls=%async_computation.2 | async-start | bytes 131072 | tf_op jit(solution)/shard_map/all_to_all | solution.py:97
Sparse Core Ops, SparseCore 0:
  84.3 193.9 all-gather.1
where the time goes:
time: 765 us
  starting transfers between devices  294 us (38%)
  waiting for transfers between devices  210 us (27%)
  blocking collectives  164 us (21%)
  local copies, waits for them, and re-layouts  54.9 us (7%)
  between operations  14.2 us (2%)
  other arithmetic  13.9 us (2%)
  matrix products  12.9 us (2%)
    all_to_all x1, starting transfers between devices, per_device(): lax.all_to_all(partial_value.reshape(workers, ROW_DEV), 'tile', split_axi...  275 us
    all_gather x1, waiting for transfers between devices, per_device(): lax.all_gather(ordered, 'tile', axis=0, tiled=True)  174 us
    all_to_all x1, blocking collectives, per_device(): lax.all_to_all(answers, ('owner', 'tile'), split_axis=0, concat_axis=0, t...  145 us
    all_to_all x1, waiting for transfers between devices, per_device(): lax.all_to_all(send_rows, ('owner', 'tile'), split_axis=0, concat_axis=0,...  29.1 us
    all_gather x1, blocking collectives, per_device(): lax.all_gather(row_cluster, 'tile', axis=0, tiled=True)  18.9 us
  transfers between devices with their start and end apart: 4, of which 4 were waited for; matrix products, arithmetic and copies ran while one was open for 1% of the time, Pallas kernels for 0%

commit v1 on v0

v1 whole, which is shorter than its diff:
```python
import functools

import jax
import jax.numpy as jnp
from jax import lax
from jax.experimental import pallas as pl
from jax.experimental.pallas import tpu as pltpu
from jax.sharding import PartitionSpec as P

D = 1024
BLK = 128
ROWS = 1024
DEVS = 128
PAIR = ROWS // DEVS
WIDE = D + 128
CHUNK = 256
CHUNKS = ROWS // CHUNK
SLOTS = 6
F32 = jnp.float32
BF16 = jnp.bfloat16
MESH = pl.DeviceIdType.MESH
NT = (((1,), (1,)), ((), ()))
HIGH = lax.Precision.HIGHEST


def place(part):
    core = part // 64
    y = (2 * ((part // 32) % 2) + (part // 2) % 2 + core) % 4
    z = (2 * ((part // 16) % 2) + part % 2 + core) % 4
    x = (part // 4) % 4
    return y * 2 + core, z * 4 + x


def part_of(owner, tile):
    core = owner % 2
    y = (owner // 2 + 4 - core) % 4
    z = (tile // 4 + 4 - core) % 4
    x = tile % 4
    return core * 64 + (y // 2) * 32 + (z // 2) * 16 + x * 4 + (y % 2) * 2 + z % 2


def iota(shape, dim):
    return lax.broadcasted_iota(jnp.int32, shape, dim)


def column(row):
    return jnp.broadcast_to(row, (128, row.shape[1])).T


def kernel(
    x_ref,
    pos_ref,
    bc_ref,
    out_ref,
    unit,
    posc,
    send,
    recv,
    parts,
    bc_here,
    bc_got,
    pos_row,
    clr,
    clc,
    acc,
    acc_got,
    ret_send,
    ret_got,
    rank_ref,
    send_sem,
    recv_sem,
    bc_sem,
    copy_send,
    copy_recv,
    cl_send,
    cl_recv,
    acc_send,
    acc_recv,
    ret_sems,
    local_sem,
):
    owner, tile = lax.axis_index("owner"), lax.axis_index("tile")
    me = part_of(owner, tile)
    core = owner % 2
    x = (me // 4) % 4
    q = me % 4
    base = me - me % 16
    barrier = pltpu.get_barrier_semaphore()

    @pl.loop(1, DEVS)
    def _(k):
        o, t = place((me + k) % DEVS)
        pl.semaphore_signal(barrier, inc=1, device_id=(o, t), device_id_type=MESH)

    pos = pos_ref[...]
    posf = pos.astype(F32)
    posc[...] = column(posf)
    for t in range(ROWS // 128):
        here = posf[:, t * 128 : (t + 1) * 128]
        less = jnp.where(posc[...] < here, 1.0, 0.0)
        rank_ref[:, t * 128 : (t + 1) * 128] = jnp.sum(less, axis=0, keepdims=True).astype(jnp.int32)

    @pl.loop(0, ROWS // 128)
    def _(c):
        rows = pl.ds(pl.multiple_of(c * 128, 128), 128)
        v = x_ref[rows, :].astype(F32)
        s = lax.rsqrt(jnp.sum(v * v, axis=1, keepdims=True) + 1e-06)
        unit[rows, :D] = (v * s).astype(BF16)
        inside = posc[rows, :].astype(jnp.int32) % ROWS
        lane = iota((128, 128), 1)
        meta = jnp.where(lane == 0, inside // 32, jnp.where(lane == 1, inside % 32, 0))
        unit[rows, D:] = meta.astype(F32).astype(BF16)

    @pl.loop(0, CHUNKS)
    def _(c):
        pick = jnp.where(rank_ref[...] == iota((CHUNK, ROWS), 0) + c * CHUNK, 1.0, 0.0).astype(BF16)
        got = jnp.dot(pick, unit[...], preferred_element_type=F32)
        blocks = CHUNK // PAIR
        send[pl.ds(c * blocks, blocks)] = got.reshape(blocks, PAIR, WIDE).astype(BF16)

    for b in range(ROWS // BLK):
        bc_here[b : b + 1, :] = jnp.full((1, 128), bc_ref[b], jnp.int32).astype(F32)

    pl.semaphore_wait(barrier, DEVS - 1)

    listed = owner * 16 + tile

    @pl.when(listed != me)
    def _():
        pltpu.make_async_remote_copy(
            bc_here, bc_got, bc_sem.at[0], bc_sem.at[1], device_id=place(listed), device_id_type=MESH
        ).start()

    @pl.when(listed == me)
    def _():
        pltpu.make_async_copy(bc_here, bc_got, bc_sem.at[1]).start()

    own = pltpu.make_async_copy(send.at[me], recv.at[me], local_sem)
    own.start()

    @pl.loop(1, DEVS)
    def _(k):
        to = (me + k * 37) % DEVS
        pltpu.make_async_remote_copy(
            send.at[to], recv.at[me], send_sem, recv_sem, device_id=place(to), device_id_type=MESH
        ).start()

    pltpu.make_async_copy(bc_here, bc_got, bc_sem.at[1]).wait()

    @pl.when(listed != me)
    def _():
        pltpu.make_async_copy(bc_here, bc_got, bc_sem.at[0]).wait()

    own.wait()
    pltpu.make_async_copy(send.at[pl.ds(0, DEVS - 1)], recv.at[pl.ds(0, DEVS - 1)], recv_sem).wait()

    step = jnp.where(core == 0, 1, 3)
    back = base + ((x + 4 - step) % 4) * 4 + q
    back2 = base + ((x + 2) % 4) * 4 + q
    ahead = base + ((x + step) % 4) * 4 + q
    flip_y = me - q + (q + 2) % 4
    flip_z = me - q + (q // 2) * 2 + (q + 1) % 2
    flip_yz = me - q + 3 - q

    def part_copy(src, c, dst, to):
        rows = pl.ds(c * CHUNK, CHUNK)
        return pltpu.make_async_remote_copy(
            parts.at[src, rows],
            parts.at[dst, rows],
            copy_send.at[dst, c],
            copy_recv.at[dst, c],
            device_id=place(to),
            device_id_type=MESH,
        )

    def arrived(slot, c):
        rows = pl.ds(c * CHUNK, CHUNK)
        pltpu.make_async_copy(parts.at[slot, rows], parts.at[slot, rows], copy_recv.at[slot, c]).wait()

    for c in range(CHUNKS):
        rows = pl.ds(c * CHUNK, CHUNK)
        blocks = CHUNK // PAIR
        parts[0, rows, :] = (
            recv[pl.ds(c * blocks, blocks), :, :D].astype(F32).reshape(CHUNK, D).astype(BF16)
        )
        for dst, to in ((1, back), (3, flip_y), (4, flip_z)):
            part_copy(0, c, dst, to).start()
        meta = recv[pl.ds(c * blocks, blocks), :, D:].astype(F32).reshape(CHUNK, 128).T
        pos_row[:, rows] = jnp.broadcast_to(meta[0:1] * 32.0 + meta[1:2], (8, CHUNK))

    inside = pos_row[...].astype(jnp.int32) // BLK
    own_cl = jnp.zeros((1, ROWS), F32)
    for b in range(ROWS // BLK):
        own_cl = own_cl + jnp.where(inside[0:1] == b, bc_got[b : b + 1, 0:1], 0.0)
    clr[0] = jnp.broadcast_to(own_cl, (8, ROWS))
    for dst, to in ((1, back), (2, back2), (3, flip_y), (4, flip_z), (5, flip_yz)):
        pltpu.make_async_remote_copy(
            clr.at[0], clr.at[dst], cl_send.at[dst], cl_recv.at[dst], device_id=place(to), device_id_type=MESH
        ).start()
    clc[0] = column(own_cl)
    posc[...] = column(pos_row[0:1])
    for m in range(SLOTS):
        acc[m] = jnp.full((8, ROWS), -1.0, F32)

    def fold(s, mask, hi, cols):
        kept = jnp.where(mask, s, -1.0)
        top = jnp.max(kept.reshape(kept.shape[0] // 8, 8, kept.shape[1]), axis=0)
        acc[hi, :, cols] = jnp.maximum(acc[hi, :, cols], top)

    def half_pair(lo, hi, h, n, diag=False):
        rows = pl.ds(pl.multiple_of(h * 512, 512), 512)
        cols = pl.ds(pl.multiple_of(n * CHUNK, CHUNK), CHUNK)
        s = lax.dot_general(parts[lo, rows, :], parts[hi, cols, :], NT, preferred_element_type=F32)
        for half in range(CHUNK // 128):
            at = pl.ds(pl.multiple_of(n * CHUNK + half * 128, 128), 128)
            mask = clc[lo, rows, :] == clr[hi, 0:1, at]
            if diag:
                mask = mask & (posc[rows, :] < pos_row[0:1, at])
            fold(s[:, half * 128 : (half + 1) * 128], mask, hi, at)

    def cl_arrived(slot):
        pltpu.make_async_copy(clr.at[slot], clr.at[slot], cl_recv.at[slot]).wait()
        clc[slot] = column(clr[slot, 0:1])

    @pl.loop(0, 2 * CHUNKS)
    def _(i):
        half_pair(0, 0, i % 2, i // 2, diag=True)

    for slot in (1, 3, 4, 5, 2):
        cl_arrived(slot)

    for c in range(CHUNKS):
        arrived(1, c)
        part_copy(1, c, 2, back).start()
        arrived(3, c)
        if c < CHUNKS // 2:
            part_copy(3, c, 5, flip_z).start()
        arrived(4, c)
        if c >= CHUNKS // 2:
            part_copy(4, c, 5, flip_y).start()

    ahead_hi = (x + step) % 4 > x

    def with_ahead(face):
        lo = jnp.where(ahead_hi, face, 1)
        hi = jnp.where(ahead_hi, 1, face)

        @pl.loop(0, 2 * CHUNKS)
        def _(i):
            half_pair(lo, hi, i % 2, i // 2)

    def with_own(slot, mine_lo):
        lo = jnp.where(mine_lo, 0, slot)
        hi = jnp.where(mine_lo, slot, 0)
        h = jnp.where(mine_lo, 0, 1)

        @pl.loop(0, CHUNKS)
        def _(n):
            half_pair(lo, hi, h, n)

    with_ahead(0)
    with_ahead(3)
    with_ahead(4)
    with_own(3, flip_y > me)
    with_own(4, flip_z > me)
    for c in range(CHUNKS):
        arrived(5, c)
    with_ahead(5)
    with_own(5, flip_yz > me)
    for c in range(CHUNKS):
        arrived(2, c)
    low = x < 2

    @pl.loop(0, CHUNKS)
    def _(n):
        for face in (0, 3, 4, 5):
            half_pair(jnp.where(low, face, 2), jnp.where(low, 2, face), jnp.where(low, 0, 1), n)

    for dst, to in ((1, ahead), (2, back2), (3, flip_y), (4, flip_z), (5, flip_yz)):
        pltpu.make_async_remote_copy(
            acc.at[dst],
            acc_got.at[dst - 1],
            acc_send.at[dst],
            acc_recv.at[dst],
            device_id=place(to),
            device_id_type=MESH,
        ).start()
    best = acc[0]
    for m in range(1, SLOTS):
        pltpu.make_async_copy(acc_got.at[m - 1], acc_got.at[m - 1], acc_recv.at[m]).wait()
        best = jnp.maximum(best, acc_got[m - 1])
    best = jnp.max(best, axis=0, keepdims=True)

    spread = jnp.where(iota((DEVS, ROWS), 1) // PAIR == iota((DEVS, ROWS), 0), best, 0.0)
    fold8 = jnp.where(iota((ROWS, 128), 0) % PAIR == iota((ROWS, 128), 1), 1.0, 0.0)
    ret = jnp.dot(spread, fold8, precision=HIGH, preferred_element_type=F32)
    ret_send[...] = ret.reshape(DEVS, 1, 128)
    back_own = pltpu.make_async_copy(ret_send.at[me], ret_got.at[me], local_sem)
    back_own.start()

    @pl.loop(1, DEVS)
    def _(k):
        to = (me + k * 37) % DEVS
        pltpu.make_async_remote_copy(
            ret_send.at[to],
            ret_got.at[me],
            ret_sems.at[0],
            ret_sems.at[1],
            device_id=place(to),
            device_id_type=MESH,
        ).start()

    back_own.wait()
    most = pl.ds(0, DEVS - 1)
    pltpu.make_async_copy(ret_send.at[most], ret_got.at[most], ret_sems.at[1]).wait()
    got = ret_got[...].reshape(DEVS, 128)
    rank = rank_ref[...]
    turn = jnp.where(rank % PAIR == iota((128, ROWS), 0), 1.0, 0.0)
    rows = jnp.dot(got, turn, precision=HIGH, preferred_element_type=F32)
    out_ref[...] = jnp.sum(
        jnp.where(rank // PAIR == iota((DEVS, ROWS), 0), rows, 0.0), axis=0, keepdims=True
    )

    pltpu.make_async_copy(send.at[most], recv.at[most], send_sem).wait()
    pltpu.make_async_copy(ret_send.at[most], ret_got.at[most], ret_sems.at[0]).wait()
    for c in range(CHUNKS):
        rows = pl.ds(c * CHUNK, CHUNK)
        for dst in range(1, SLOTS):
            pltpu.make_async_copy(parts.at[0, rows], parts.at[dst, rows], copy_send.at[dst, c]).wait()
    for dst in range(1, SLOTS):
        pltpu.make_async_copy(clr.at[0], clr.at[dst], cl_send.at[dst]).wait()
        pltpu.make_async_copy(acc.at[dst], acc_got.at[dst - 1], acc_send.at[dst]).wait()


def per_device(embeddings, sorted_pos, block_cluster, tile_list):
    del tile_list
    vmem = pl.BlockSpec(memory_space=pltpu.VMEM)
    out = pl.pallas_call(
        kernel,
        out_shape=jax.ShapeDtypeStruct((1, ROWS), F32),
        in_specs=[vmem, vmem, pl.BlockSpec(memory_space=pltpu.SMEM)],
        out_specs=vmem,
        scratch_shapes=[
            pltpu.VMEM((ROWS, WIDE), BF16),
            pltpu.VMEM((ROWS, 128), F32),
            pltpu.VMEM((DEVS, PAIR, WIDE), BF16),
            pltpu.VMEM((DEVS, PAIR, WIDE), BF16),
            pltpu.VMEM((SLOTS, ROWS, D), BF16),
            pltpu.VMEM((8, 128), F32),
            pltpu.VMEM((8, 128), F32),
            pltpu.VMEM((8, ROWS), F32),
            pltpu.VMEM((SLOTS, 8, ROWS), F32),
            pltpu.VMEM((SLOTS, ROWS, 128), F32),
            pltpu.VMEM((SLOTS, 8, ROWS), F32),
            pltpu.VMEM((SLOTS - 1, 8, ROWS), F32),
            pltpu.VMEM((DEVS, 1, 128), F32),
            pltpu.VMEM((DEVS, 1, 128), F32),
            pltpu.VMEM((1, ROWS), jnp.int32),
            pltpu.SemaphoreType.DMA,
            pltpu.SemaphoreType.DMA,
            pltpu.SemaphoreType.DMA((2,)),
            pltpu.SemaphoreType.DMA((SLOTS, CHUNKS)),
            pltpu.SemaphoreType.DMA((SLOTS, CHUNKS)),
            pltpu.SemaphoreType.DMA((SLOTS,)),
            pltpu.SemaphoreType.DMA((SLOTS,)),
            pltpu.SemaphoreType.DMA((SLOTS,)),
            pltpu.SemaphoreType.DMA((SLOTS,)),
            pltpu.SemaphoreType.DMA((2,)),
            pltpu.SemaphoreType.DMA,
        ],
        compiler_params=pltpu.CompilerParams(
            collective_id=0, has_side_effects=True, vmem_limit_bytes=56 * 1024 * 1024
        ),
    )(embeddings, sorted_pos.reshape(1, ROWS), block_cluster)
    return out.reshape(ROWS)


def solution(mesh):
    placed = (
        P(("owner", "tile"), None),
        P(("owner", "tile")),
        P(("owner", "tile")),
        P("owner", "tile", None, None),
    )
    return jax.shard_map(
        per_device, mesh=mesh, in_specs=placed, out_specs=P(("owner", "tile")), check_vma=False
    )
```

time: 765 us -> 125 us (0.16)
  starting transfers between devices: 294 us -> 0 us
  waiting for transfers between devices: 210 us -> 0 us
  blocking collectives: 164 us -> 0 us
  Pallas kernels: 0 us -> 124 us
  local copies, waits for them, and re-layouts: 54.9 us -> 1.28 us
  between operations: 14.2 us -> 0.01 us
  other arithmetic: 13.9 us -> 0 us
  matrix products: 12.9 us -> 0 us
    all_to_all x3 -> x0, starting transfers between devices: 294 us -> none  [the longest x1 275 us: per_device(): lax.all_to_all(partial_value.reshape(workers, ROW_DEV), 'tile', split_axi...]
    all_gather x1 -> x0, waiting for transfers between devices: 174 us -> none  [per_device(): lax.all_gather(ordered, 'tile', axis=0, tiled=True)]
    all_to_all x1 -> x0, blocking collectives: 145 us -> none  [per_device(): lax.all_to_all(answers, ('owner', 'tile'), split_axis=0, concat_axis=0, t...]
    pallas_call x0 -> x1, Pallas kernels: none -> 124 us  [per_device(): pl.pallas_call(kernel, out_shape=jax.ShapeDtypeStruct((1, ROWS), F32), in...]
    gather x9 -> x0, local copies, waits for them, and re-layouts: 40.6 us -> none  [the longest x1 11.1 us: advance(): queries = query_blocks[row_ids]]
    all_to_all x3 -> x0, waiting for transfers between devices: 36.8 us -> none  [the longest x1 29.1 us: per_device(): lax.all_to_all(send_rows, ('owner', 'tile'), split_axis=0, concat_axis=0,...]
    all_gather x1 -> x0, blocking collectives: 18.9 us -> none  [per_device(): lax.all_gather(row_cluster, 'tile', axis=0, tiled=True)]
    dot_general x1 -> x0, matrix products: 12.9 us -> none  [advance(): jnp.einsum('tid,tjd->tij', queries, columns, preferred_element_type=jnp.f...]
  transfers between devices with their start and end apart: 4 -> 0, of which waited for: 4 -> 0; matrix products, arithmetic and copies ran while one was open for 1% -> 0% of each run, Pallas kernels for 0% -> 0%
where the time goes in v1:
time: 125 us
  Pallas kernels  124 us (99%)
  local copies, waits for them, and re-layouts  1.28 us (1%)
    pallas_call x1, Pallas kernels, per_device(): pl.pallas_call(kernel, out_shape=jax.ShapeDtypeStruct((1, ROWS), F32), in...  124 us

profile of v1, /device:TPU:1, one launch (start us, length us, event | category | flops | bytes accessed | tf_op | source)
XLA Modules:
  0.0 125.1 jit_solution(3679828641559013813)
XLA Ops:
  0.0 123.8 %shard_map.37 = f32[1,1024]{1,0:T(1,128)} custom-call(bf16[1024,1024]{1,0:T(8,128)(2,1)} %x_ref.1, s32[1,1024]{1,0:T(1,128)} %bitcast.3, s32[8]{0:T(128)} %bc_ref.1), custom_call_target="tpu_custom_call" | custom-call | tf_op jit(solution)/shard_map/pallas_call | solution.py:338
  123.8 1.3 %copy.5 = f32[1024]{0:T(1024)} copy(f32[1024]{0:T(1024)} %bitcast.2) | data formatting | bytes 8192

commit v2 on v1

v2 whole, which is shorter than its diff:
```python
import functools

import jax
import jax.numpy as jnp
from jax import lax
from jax.experimental import pallas as pl
from jax.experimental.pallas import tpu as pltpu
from jax.sharding import PartitionSpec as P

D = 1024
BLK = 128
ROWS = 1024
DEVS = 128
PAIR = ROWS // DEVS
CHUNK = 256
CHUNKS = ROWS // CHUNK
SLOTS = 6
F32 = jnp.float32
BF16 = jnp.bfloat16
MESH = pl.DeviceIdType.MESH
NT = (((1,), (1,)), ((), ()))
HIGH = lax.Precision.HIGHEST


def place(part):
    core = part // 64
    y = (2 * ((part // 32) % 2) + (part // 2) % 2 + core) % 4
    z = (2 * ((part // 16) % 2) + part % 2 + core) % 4
    x = (part // 4) % 4
    return y * 2 + core, z * 4 + x


def part_of(owner, tile):
    core = owner % 2
    y = (owner // 2 + 4 - core) % 4
    z = (tile // 4 + 4 - core) % 4
    x = tile % 4
    return core * 64 + (y // 2) * 32 + (z // 2) * 16 + x * 4 + (y % 2) * 2 + z % 2


def all_to_all(src, dst, me, core, y, z, x, send_sem, recv_sem):
    rows = [(core + d) % 2 for d in range(2)]
    ys = [(y + d) % 4 for d in range(4)]
    zs = [(z + d) % 4 for d in range(4)]
    xs = [(x + d) % 4 for d in range(4)]
    for k in range(1, DEVS):
        j = k * 37 % DEVS
        c, yy, zz, xx = rows[j // 64], ys[j // 16 % 4], zs[j // 4 % 4], xs[j % 4]
        o, t = yy * 2 + c, zz * 4 + xx
        pltpu.make_async_remote_copy(
            src.at[part_of(o, t)],
            dst.at[me],
            send_sem,
            recv_sem,
            device_id=(o, t),
            device_id_type=MESH,
        ).start()


def iota(shape, dim):
    return lax.broadcasted_iota(jnp.int32, shape, dim)


def column(row):
    return jnp.broadcast_to(row, (128, row.shape[1])).T


def kernel(
    x_ref,
    pos_ref,
    bc_ref,
    out_ref,
    unit,
    posc,
    send,
    recv,
    parts,
    bc_here,
    bc_got,
    pos_row,
    clr,
    clc,
    acc,
    acc_got,
    small_send,
    small_got,
    ret_got,
    rank_ref,
    send_sem,
    recv_sem,
    bc_sem,
    copy_send,
    copy_recv,
    cl_send,
    cl_recv,
    acc_send,
    acc_recv,
    ret_sems,
    local_sem,
    entry_sem,
    meta_sems,
):
    owner, tile = lax.axis_index("owner"), lax.axis_index("tile")
    me = part_of(owner, tile)
    core = owner % 2
    y, z, x = owner // 2, tile // 4, tile % 4
    q = me % 4
    base = me - me % 16
    barrier = pltpu.get_barrier_semaphore()

    for k in range(1, 16):
        pl.semaphore_signal(
            barrier, inc=1, device_id=(owner, (tile + k) % 16), device_id_type=MESH
        )
    for k in range(1, 8):
        pl.semaphore_signal(barrier, inc=1, device_id=((owner + k) % 8, tile), device_id_type=MESH)

    pos = pos_ref[...]
    posf = pos.astype(F32)
    posc[...] = column(posf)
    for t in range(ROWS // 128):
        here = posf[:, t * 128 : (t + 1) * 128]
        less = jnp.where(posc[...] < here, 1.0, 0.0)
        rank_ref[:, t * 128 : (t + 1) * 128] = jnp.sum(less, axis=0, keepdims=True).astype(jnp.int32)

    @pl.loop(0, ROWS // 128)
    def _(c):
        rows = pl.ds(pl.multiple_of(c * 128, 128), 128)
        v = x_ref[rows, :].astype(F32)
        s = lax.rsqrt(jnp.sum(v * v, axis=1, keepdims=True) + 1e-06)
        unit[rows, :] = (v * s).astype(BF16)

    @pl.loop(0, CHUNKS)
    def _(c):
        pick = jnp.where(rank_ref[...] == iota((CHUNK, ROWS), 0) + c * CHUNK, 1.0, 0.0).astype(BF16)
        got = jnp.dot(pick, unit[...], preferred_element_type=F32)
        blocks = CHUNK // PAIR
        send[pl.ds(c * blocks, blocks)] = got.reshape(blocks, PAIR, D).astype(BF16)

    rank = rank_ref[...]
    inside = (pos % ROWS).astype(F32)
    group = jnp.where(rank // PAIR == iota((DEVS, ROWS), 0), inside, 0.0)
    turn = jnp.where(rank % PAIR == iota((128, ROWS), 0), 1.0, 0.0)
    meta = lax.dot_general(group, turn, NT, precision=HIGH, preferred_element_type=F32)
    small_send[0] = meta.reshape(DEVS, 1, 128)

    for b in range(ROWS // BLK):
        bc_here[b : b + 1, :] = jnp.full((1, 128), bc_ref[b], jnp.int32).astype(F32)

    pl.semaphore_wait(barrier, 22)
    for k in range(1, 8):
        pl.semaphore_signal(entry_sem, inc=1, device_id=((owner + k) % 8, tile), device_id_type=MESH)
    pl.semaphore_wait(entry_sem, 7)

    listed = owner * 16 + tile

    @pl.when(listed != me)
    def _():
        pltpu.make_async_remote_copy(
            bc_here, bc_got, bc_sem.at[0], bc_sem.at[1], device_id=place(listed), device_id_type=MESH
        ).start()

    @pl.when(listed == me)
    def _():
        pltpu.make_async_copy(bc_here, bc_got, bc_sem.at[1]).start()

    own = pltpu.make_async_copy(send.at[me], recv.at[me], local_sem.at[0])
    own.start()
    own_meta = pltpu.make_async_copy(small_send.at[0, me], small_got.at[me], local_sem.at[1])
    own_meta.start()
    all_to_all(send, recv, me, core, y, z, x, send_sem, recv_sem)
    all_to_all(small_send.at[0], small_got, me, core, y, z, x, meta_sems.at[0], meta_sems.at[1])
    most = pl.ds(0, DEVS - 1)
    own.wait()
    pltpu.make_async_copy(send.at[most], recv.at[most], recv_sem).wait()

    step = jnp.where(core == 0, 1, 3)
    back = base + ((x + 4 - step) % 4) * 4 + q
    back2 = base + ((x + 2) % 4) * 4 + q
    ahead = base + ((x + step) % 4) * 4 + q
    flip_y = me - q + (q + 2) % 4
    flip_z = me - q + (q // 2) * 2 + (q + 1) % 2
    flip_yz = me - q + 3 - q

    def part_copy(src, c, dst, to):
        rows = pl.ds(c * CHUNK, CHUNK)
        return pltpu.make_async_remote_copy(
            parts.at[src, rows],
            parts.at[dst, rows],
            copy_send.at[dst, c],
            copy_recv.at[dst, c],
            device_id=place(to),
            device_id_type=MESH,
        )

    def arrived(slot, c):
        rows = pl.ds(c * CHUNK, CHUNK)
        pltpu.make_async_copy(parts.at[slot, rows], parts.at[slot, rows], copy_recv.at[slot, c]).wait()

    def ready(c):
        rows = pl.ds(c * CHUNK, CHUNK)
        blocks = CHUNK // PAIR
        parts[0, rows, :] = recv[pl.ds(c * blocks, blocks)].astype(F32).reshape(CHUNK, D).astype(BF16)
        for dst, to in ((1, back), (3, flip_y), (4, flip_z)):
            part_copy(0, c, dst, to).start()

    ready(0)
    own_meta.wait()
    pltpu.make_async_copy(small_send.at[0, most], small_got.at[most], meta_sems.at[1]).wait()
    pltpu.make_async_copy(bc_here, bc_got, bc_sem.at[1]).wait()

    @pl.when(listed != me)
    def _():
        pltpu.make_async_copy(bc_here, bc_got, bc_sem.at[0]).wait()

    got = small_got[...].reshape(DEVS, 128)
    turn = jnp.where(iota((128, ROWS), 1) % PAIR == iota((128, ROWS), 0), 1.0, 0.0)
    at_row = jnp.dot(got, turn, precision=HIGH, preferred_element_type=F32)
    at_row = jnp.where(iota((DEVS, ROWS), 1) // PAIR == iota((DEVS, ROWS), 0), at_row, 0.0)
    own_pos = jnp.sum(at_row, axis=0, keepdims=True)
    pos_row[...] = jnp.broadcast_to(own_pos, (8, ROWS))
    block = own_pos.astype(jnp.int32) // BLK
    own_cl = jnp.zeros((1, ROWS), F32)
    for b in range(ROWS // BLK):
        own_cl = own_cl + jnp.where(block == b, bc_got[b : b + 1, 0:1], 0.0)
    clr[0] = jnp.broadcast_to(own_cl, (8, ROWS))
    for dst, to in ((1, back), (2, back2), (3, flip_y), (4, flip_z), (5, flip_yz)):
        pltpu.make_async_remote_copy(
            clr.at[0], clr.at[dst], cl_send.at[dst], cl_recv.at[dst], device_id=place(to), device_id_type=MESH
        ).start()
    for c in range(1, CHUNKS):
        ready(c)
    clc[0] = column(own_cl)
    posc[...] = column(pos_row[0:1])
    for m in range(SLOTS):
        acc[m] = jnp.full((8, ROWS), -1.0, F32)

    def fold(s, mask, hi, cols):
        kept = jnp.where(mask, s, -1.0)
        top = jnp.max(kept.reshape(kept.shape[0] // 8, 8, kept.shape[1]), axis=0)
        acc[hi, :, cols] = jnp.maximum(acc[hi, :, cols], top)

    def block_pair(lo, row, m, hi, col, n, diag=False):
        rows = pl.ds(pl.multiple_of(row, m), m)
        cols = pl.ds(pl.multiple_of(col, n), n)
        s = lax.dot_general(parts[lo, rows, :], parts[hi, cols, :], NT, preferred_element_type=F32)
        for k in range(n // 128):
            at = pl.ds(pl.multiple_of(col + k * 128, 128), 128)
            mask = clc[lo, rows, :] == clr[hi, 0:1, at]
            if diag:
                mask = mask & (posc[rows, :] < pos_row[0:1, at])
            fold(s[:, k * 128 : (k + 1) * 128], mask, hi, at)

    def cl_arrived(slot):
        pltpu.make_async_copy(clr.at[slot], clr.at[slot], cl_recv.at[slot]).wait()
        clc[slot] = column(clr[slot, 0:1])

    low = x < 2

    def forward(c):
        arrived(1, c)
        if c < CHUNKS // 2:

            @pl.when((x + 4 - step) % 4 < 2)
            def _():
                part_copy(1, c, 2, back).start()
        else:
            part_copy(1, c, 2, back).start()
        arrived(3, c)
        if c < CHUNKS // 2:
            part_copy(3, c, 5, flip_z).start()
        arrived(4, c)
        if c >= CHUNKS // 2:
            part_copy(4, c, 5, flip_y).start()

    forward(0)

    @pl.loop(0, 2)
    def _(i):
        block_pair(0, 0, ROWS, 0, i * 512, 512, diag=True)

    forward(1)
    for slot in (1, 3, 4):
        cl_arrived(slot)
    forward(2)
    for slot in (5, 2):
        cl_arrived(slot)
    forward(3)

    ahead_hi = (x + step) % 4 > x

    def with_ahead(face):
        lo = jnp.where(ahead_hi, face, 1)
        hi = jnp.where(ahead_hi, 1, face)

        @pl.loop(0, 2)
        def _(i):
            block_pair(lo, 0, ROWS, hi, i * 512, 512)

    def with_own(slot, mine_lo):
        lo = jnp.where(mine_lo, 0, slot)
        hi = jnp.where(mine_lo, slot, 0)
        block_pair(lo, jnp.where(mine_lo, 0, 512), 512, hi, 0, ROWS)

    with_ahead(0)
    with_ahead(3)
    with_ahead(4)
    with_own(3, flip_y > me)
    with_own(4, flip_z > me)
    for c in range(CHUNKS):
        arrived(5, c)
    with_ahead(5)
    with_own(5, flip_yz > me)

    for n in range(CHUNKS):
        if n < CHUNKS // 2:

            @pl.when(low)
            def _():
                arrived(2, n)

        else:
            arrived(2, n)

        @pl.when(low)
        def _():
            for face in (0, 3, 4, 5):
                block_pair(face, 0, 512, 2, n * CHUNK, CHUNK)

    @pl.when(jnp.logical_not(low))
    def _():
        for face in (0, 3, 4, 5):
            block_pair(2, 512, 512, face, 0, ROWS)

    for dst, to in ((1, ahead), (2, back2), (3, flip_y), (4, flip_z), (5, flip_yz)):
        pltpu.make_async_remote_copy(
            acc.at[dst],
            acc_got.at[dst - 1],
            acc_send.at[dst],
            acc_recv.at[dst],
            device_id=place(to),
            device_id_type=MESH,
        ).start()
    best = acc[0]
    for m in range(1, SLOTS):
        pltpu.make_async_copy(acc_got.at[m - 1], acc_got.at[m - 1], acc_recv.at[m]).wait()
        best = jnp.maximum(best, acc_got[m - 1])
    best = jnp.max(best, axis=0, keepdims=True)

    spread = jnp.where(iota((DEVS, ROWS), 1) // PAIR == iota((DEVS, ROWS), 0), best, 0.0)
    fold8 = jnp.where(iota((ROWS, 128), 0) % PAIR == iota((ROWS, 128), 1), 1.0, 0.0)
    ret = jnp.dot(spread, fold8, precision=HIGH, preferred_element_type=F32)
    small_send[1] = ret.reshape(DEVS, 1, 128)
    back_own = pltpu.make_async_copy(small_send.at[1, me], ret_got.at[me], local_sem.at[0])
    back_own.start()

    all_to_all(small_send.at[1], ret_got, me, core, y, z, x, ret_sems.at[0], ret_sems.at[1])
    back_own.wait()
    pltpu.make_async_copy(small_send.at[1, most], ret_got.at[most], ret_sems.at[1]).wait()
    got = ret_got[...].reshape(DEVS, 128)
    rank = rank_ref[...]
    turn = jnp.where(rank % PAIR == iota((128, ROWS), 0), 1.0, 0.0)
    rows = jnp.dot(got, turn, precision=HIGH, preferred_element_type=F32)
    out_ref[...] = jnp.sum(
        jnp.where(rank // PAIR == iota((DEVS, ROWS), 0), rows, 0.0), axis=0, keepdims=True
    )

    pltpu.make_async_copy(send.at[most], recv.at[most], send_sem).wait()
    pltpu.make_async_copy(small_send.at[0, most], small_got.at[most], meta_sems.at[0]).wait()
    pltpu.make_async_copy(small_send.at[1, most], ret_got.at[most], ret_sems.at[0]).wait()
    for c in range(CHUNKS):
        rows = pl.ds(c * CHUNK, CHUNK)
        for dst in (1, 3, 4, 5):
            pltpu.make_async_copy(parts.at[0, rows], parts.at[dst, rows], copy_send.at[dst, c]).wait()

        @pl.when(((x + 4 - step) % 4 < 2) | (c >= CHUNKS // 2))
        def _():
            pltpu.make_async_copy(parts.at[1, rows], parts.at[2, rows], copy_send.at[2, c]).wait()

    for dst in range(1, SLOTS):
        pltpu.make_async_copy(clr.at[0], clr.at[dst], cl_send.at[dst]).wait()
        pltpu.make_async_copy(acc.at[dst], acc_got.at[dst - 1], acc_send.at[dst]).wait()


def per_device(embeddings, sorted_pos, block_cluster, tile_list):
    del tile_list
    vmem = pl.BlockSpec(memory_space=pltpu.VMEM)
    out = pl.pallas_call(
        kernel,
        out_shape=jax.ShapeDtypeStruct((1, ROWS), F32),
        in_specs=[vmem, vmem, pl.BlockSpec(memory_space=pltpu.SMEM)],
        out_specs=vmem,
        scratch_shapes=[
            pltpu.VMEM((ROWS, D), BF16),
            pltpu.VMEM((ROWS, 128), F32),
            pltpu.VMEM((DEVS, PAIR, D), BF16),
            pltpu.VMEM((DEVS, PAIR, D), BF16),
            pltpu.VMEM((SLOTS, ROWS, D), BF16),
            pltpu.VMEM((8, 128), F32),
            pltpu.VMEM((8, 128), F32),
            pltpu.VMEM((8, ROWS), F32),
            pltpu.VMEM((SLOTS, 8, ROWS), F32),
            pltpu.VMEM((SLOTS, ROWS, 128), F32),
            pltpu.VMEM((SLOTS, 8, ROWS), F32),
            pltpu.VMEM((SLOTS - 1, 8, ROWS), F32),
            pltpu.VMEM((2, DEVS, 1, 128), F32),
            pltpu.VMEM((DEVS, 1, 128), F32),
            pltpu.VMEM((DEVS, 1, 128), F32),
            pltpu.VMEM((1, ROWS), jnp.int32),
            pltpu.SemaphoreType.DMA,
            pltpu.SemaphoreType.DMA,
            pltpu.SemaphoreType.DMA((2,)),
            pltpu.SemaphoreType.DMA((SLOTS, CHUNKS)),
            pltpu.SemaphoreType.DMA((SLOTS, CHUNKS)),
            pltpu.SemaphoreType.DMA((SLOTS,)),
            pltpu.SemaphoreType.DMA((SLOTS,)),
            pltpu.SemaphoreType.DMA((SLOTS,)),
            pltpu.SemaphoreType.DMA((SLOTS,)),
            pltpu.SemaphoreType.DMA((2,)),
            pltpu.SemaphoreType.DMA((2,)),
            pltpu.SemaphoreType.REGULAR,
            pltpu.SemaphoreType.DMA((2,)),
        ],
        compiler_params=pltpu.CompilerParams(
            collective_id=0, has_side_effects=True, vmem_limit_bytes=56 * 1024 * 1024
        ),
    )(embeddings, sorted_pos.reshape(1, ROWS), block_cluster)
    return out.reshape(ROWS)


def solution(mesh):
    placed = (
        P(("owner", "tile"), None),
        P(("owner", "tile")),
        P(("owner", "tile")),
        P("owner", "tile", None, None),
    )
    return jax.shard_map(
        per_device, mesh=mesh, in_specs=placed, out_specs=P(("owner", "tile")), check_vma=False
    )
```

time: 125 us -> 105 us (0.84)
  Pallas kernels: 124 us -> 104 us
    pallas_call x1, Pallas kernels: 124 us -> 104 us  [per_device(): pl.pallas_call(kernel, out_shape=jax.ShapeDtypeStruct((1, ROWS), F32), in...]
where the time goes in v2:
time: 105 us
  Pallas kernels  104 us (99%)
  local copies, waits for them, and re-layouts  1.28 us (1%)
    pallas_call x1, Pallas kernels, per_device(): pl.pallas_call(kernel, out_shape=jax.ShapeDtypeStruct((1, ROWS), F32), in...  104 us

profile of v2, /device:TPU:1, one launch (start us, length us, event | category | flops | bytes accessed | tf_op | source)
XLA Modules:
  0.0 105.1 jit_solution(3650327920802995983)
XLA Ops:
  0.0 103.8 %shard_map.37 = f32[1,1024]{1,0:T(1,128)} custom-call(bf16[1024,1024]{1,0:T(8,128)(2,1)} %x_ref.1, s32[1,1024]{1,0:T(1,128)} %bitcast.3, s32[8]{0:T(128)} %bc_ref.1), custom_call_target="tpu_custom_call" | custom-call | tf_op jit(solution)/shard_map/pallas_call | solution.py:388
  103.8 1.3 %copy.5 = f32[1024]{0:T(1024)} copy(f32[1024]{0:T(1024)} %bitcast.2) | data formatting | bytes 8192

commit v3 on v2

--- a/solution.py
+++ b/solution.py
@@ -1,5 +1,3 @@
-import functools
-
 import jax
 import jax.numpy as jnp
 from jax import lax
@@ -19,7 +17,6 @@
 BF16 = jnp.bfloat16
 MESH = pl.DeviceIdType.MESH
 NT = (((1,), (1,)), ((), ()))
-HIGH = lax.Precision.HIGHEST
 
 
 def place(part):
@@ -38,27 +35,53 @@
     return core * 64 + (y // 2) * 32 + (z // 2) * 16 + x * 4 + (y % 2) * 2 + z % 2
 
 
-def all_to_all(src, dst, me, core, y, z, x, send_sem, recv_sem):
-    rows = [(core + d) % 2 for d in range(2)]
-    ys = [(y + d) % 4 for d in range(4)]
-    zs = [(z + d) % 4 for d in range(4)]
-    xs = [(x + d) % 4 for d in range(4)]
-    for k in range(1, DEVS):
-        j = k * 37 % DEVS
-        c, yy, zz, xx = rows[j // 64], ys[j // 16 % 4], zs[j // 4 % 4], xs[j % 4]
-        o, t = yy * 2 + c, zz * 4 + xx
-        pltpu.make_async_remote_copy(
-            src.at[part_of(o, t)],
-            dst.at[me],
-            send_sem,
-            recv_sem,
-            device_id=(o, t),
-            device_id_type=MESH,
-        ).start()
-
-
 def iota(shape, dim):
     return lax.broadcasted_iota(jnp.int32, shape, dim)
+
+
+def rows_then_columns(sent, mid, got, owner, tile, sems, local):
+    def first():
+        stay = pltpu.make_async_copy(sent.at[owner], mid.at[owner], local.at[0])
+        stay.start()
+        for k in range(1, 8):
+            to = (owner + k) % 8
+            pltpu.make_async_remote_copy(
+                sent.at[to],
+                mid.at[owner],
+                sems.at[0],
+                sems.at[1],
+                device_id=(to, tile),
+                device_id_type=MESH,
+            ).start()
+
+    def second():
+        seven = pl.ds(0, 7)
+        pltpu.make_async_copy(sent.at[owner], mid.at[owner], local.at[0]).wait()
+        pltpu.make_async_copy(sent.at[seven], mid.at[seven], sems.at[1]).wait()
+        stay = pltpu.make_async_copy(mid.at[:, tile], got.at[tile], local.at[1])
+        stay.start()
+        for k in range(1, 16):
+            to = (tile + k) % 16
+            pltpu.make_async_remote_copy(
+                mid.at[:, to],
+                got.at[tile],
+                sems.at[2],
+                sems.at[3],
+                device_id=(owner, to),
+                device_id_type=MESH,
+            ).start()
+
+    def arrive():
+        fifteen = pl.ds(0, 15)
+        pltpu.make_async_copy(got.at[tile], got.at[tile], local.at[1]).wait()
+        pltpu.make_async_copy(got.at[fifteen], got.at[fifteen], sems.at[3]).wait()
+
+    def left():
+        seven, fifteen = pl.ds(0, 7), pl.ds(0, 15)
+        pltpu.make_async_copy(sent.at[seven], mid.at[seven], sems.at[0]).wait()
+        pltpu.make_async_copy(got.at[fifteen], got.at[fifteen], sems.at[2]).wait()
+
+    return first, second, arrive, left
 
 
 def column(row):
@@ -82,10 +105,14 @@
     clc,
     acc,
     acc_got,
-    small_send,
-    small_got,
+    meta_send,
+    meta_mid,
+    meta_got,
+    ret_send,
     ret_got,
     rank_ref,
+    turn_ref,
+    mine_ref,
     send_sem,
     recv_sem,
     bc_sem,
@@ -96,9 +123,10 @@
     acc_send,
     acc_recv,
     ret_sems,
+    meta_sems,
     local_sem,
-    entry_sem,
-    meta_sems,
+    ret_local,
+    meta_local,
 ):
     owner, tile = lax.axis_index("owner"), lax.axis_index("tile")
     me = part_of(owner, tile)
@@ -108,20 +136,21 @@
     base = me - me % 16
     barrier = pltpu.get_barrier_semaphore()
 
-    for k in range(1, 16):
-        pl.semaphore_signal(
-            barrier, inc=1, device_id=(owner, (tile + k) % 16), device_id_type=MESH
-        )
-    for k in range(1, 8):
-        pl.semaphore_signal(barrier, inc=1, device_id=((owner + k) % 8, tile), device_id_type=MESH)
+    for k in range(1, DEVS):
+        to = ((owner + k // 16) % 8, (tile + k % 16) % 16)
+        pl.semaphore_signal(barrier, inc=1, device_id=to, device_id_type=MESH)
 
     pos = pos_ref[...]
     posf = pos.astype(F32)
     posc[...] = column(posf)
+    ranks = []
     for t in range(ROWS // 128):
         here = posf[:, t * 128 : (t + 1) * 128]
         less = jnp.where(posc[...] < here, 1.0, 0.0)
-        rank_ref[:, t * 128 : (t + 1) * 128] = jnp.sum(less, axis=0, keepdims=True).astype(jnp.int32)
+        ranks.append(jnp.sum(less, axis=0, keepdims=True).astype(jnp.int32))
+    within = jnp.concatenate(ranks, axis=1) & (PAIR - 1)
+    to_o, to_t = place(pos >> 10)
+    rank_ref[...] = (to_o * 16 + to_t) * PAIR + within
 
     @pl.loop(0, ROWS // 128)
     def _(c):
@@ -137,20 +166,23 @@
         blocks = CHUNK // PAIR
         send[pl.ds(c * blocks, blocks)] = got.reshape(blocks, PAIR, D).astype(BF16)
 
-    rank = rank_ref[...]
-    inside = (pos % ROWS).astype(F32)
-    group = jnp.where(rank // PAIR == iota((DEVS, ROWS), 0), inside, 0.0)
-    turn = jnp.where(rank % PAIR == iota((128, ROWS), 0), 1.0, 0.0)
-    meta = lax.dot_general(group, turn, NT, precision=HIGH, preferred_element_type=F32)
-    small_send[0] = meta.reshape(DEVS, 1, 128)
+    inside = pos & (ROWS - 1)
+    here = iota((DEVS, ROWS), 0) == to_o * 16 + to_t
+    high = jnp.where(here, (inside >> 5).astype(F32), 0.0).astype(BF16)
+    below = jnp.where(here, (inside & 31).astype(F32), 0.0).astype(BF16)
+    lane = iota((128, ROWS), 0)
+    turn = jnp.where(lane == within, 1.0, 0.0).astype(BF16)
+    turn2 = jnp.where(lane == within + PAIR, 1.0, 0.0).astype(BF16)
+    meta = lax.dot_general(high, turn, NT, preferred_element_type=F32)
+    meta = meta + lax.dot_general(below, turn2, NT, preferred_element_type=F32)
+    meta_send[...] = meta.reshape(8, 16, 1, 128)
+    turn_ref[...] = turn
+    mine_ref[...] = jnp.where(here, 1.0, 0.0)
 
     for b in range(ROWS // BLK):
         bc_here[b : b + 1, :] = jnp.full((1, 128), bc_ref[b], jnp.int32).astype(F32)
 
-    pl.semaphore_wait(barrier, 22)
-    for k in range(1, 8):
-        pl.semaphore_signal(entry_sem, inc=1, device_id=((owner + k) % 8, tile), device_id_type=MESH)
-    pl.semaphore_wait(entry_sem, 7)
+    pl.semaphore_wait(barrier, DEVS - 1)
 
     listed = owner * 16 + tile
 
@@ -164,16 +196,54 @@
     def _():
         pltpu.make_async_copy(bc_here, bc_got, bc_sem.at[1]).start()
 
-    own = pltpu.make_async_copy(send.at[me], recv.at[me], local_sem.at[0])
+    meta_first, meta_second, meta_arrive, meta_left = rows_then_columns(
+        meta_send, meta_mid, meta_got, owner, tile, meta_sems, meta_local
+    )
+    meta_first()
+
+    dev = owner * 16 + tile
+    own = pltpu.make_async_copy(send.at[dev], recv.at[dev], local_sem)
     own.start()
-    own_meta = pltpu.make_async_copy(small_send.at[0, me], small_got.at[me], local_sem.at[1])
-    own_meta.start()
-    all_to_all(send, recv, me, core, y, z, x, send_sem, recv_sem)
-    all_to_all(small_send.at[0], small_got, me, core, y, z, x, meta_sems.at[0], meta_sems.at[1])
-    most = pl.ds(0, DEVS - 1)
-    own.wait()
-    pltpu.make_async_copy(send.at[most], recv.at[most], recv_sem).wait()
-
+
+    def send_rows(first, last):
+        @pl.loop(first, last)
+        def _(k):
+            j = k * 37 % DEVS
+            o = (owner + j // 16) % 8
+            t = (tile // 4 + j // 4) % 4 * 4 + (tile + j) % 4
+            pltpu.make_async_remote_copy(
+                send.at[o * 16 + t],
+                recv.at[dev],
+                send_sem,
+                recv_sem,
+                device_id=(o, t),
+                device_id_type=MESH,
+            ).start()
+
+    send_rows(1, 48)
+    meta_second()
+    send_rows(48, DEVS)
+
+    meta_arrive()
+    pltpu.make_async_copy(bc_here, bc_got, bc_sem.at[1]).wait()
+
+    @pl.when(listed != me)
+    def _():
+        pltpu.make_async_copy(bc_here, bc_got, bc_sem.at[0]).wait()
+
+    got = meta_got[...].reshape(DEVS, 128).astype(BF16)
+    lane, at = iota((128, ROWS), 0), iota((128, ROWS), 1)
+    turn = jnp.where(lane == (at & 7), 32.0, jnp.where(lane == (at & 7) + PAIR, 1.0, 0.0)).astype(BF16)
+    at_row = jnp.dot(got, turn, preferred_element_type=F32)
+    source = iota((DEVS, ROWS), 1) >> 3
+    at_row = jnp.where((source & 15) * 8 + (source >> 4) == iota((DEVS, ROWS), 0), at_row, 0.0)
+    own_pos = jnp.sum(at_row, axis=0, keepdims=True)
+    pos_row[...] = jnp.broadcast_to(own_pos, (8, ROWS))
+    block = own_pos.astype(jnp.int32) >> 7
+    own_cl = jnp.zeros((1, ROWS), F32)
+    for b in range(ROWS // BLK):
+        own_cl = own_cl + jnp.where(block == b, bc_got[b : b + 1, 0:1], 0.0)
+    clr[0] = jnp.broadcast_to(own_cl, (8, ROWS))
     step = jnp.where(core == 0, 1, 3)
     back = base + ((x + 4 - step) % 4) * 4 + q
     back2 = base + ((x + 2) % 4) * 4 + q
@@ -181,6 +251,19 @@
     flip_y = me - q + (q + 2) % 4
     flip_z = me - q + (q // 2) * 2 + (q + 1) % 2
     flip_yz = me - q + 3 - q
+
+    for dst, to in ((1, back), (2, back2), (3, flip_y), (4, flip_z), (5, flip_yz)):
+        pltpu.make_async_remote_copy(
+            clr.at[0], clr.at[dst], cl_send.at[dst], cl_recv.at[dst], device_id=place(to), device_id_type=MESH
+        ).start()
+    clc[0] = column(own_cl)
+    posc[...] = column(own_pos)
+    for m in range(SLOTS):
+        acc[m] = jnp.full((8, ROWS), -1.0, F32)
+
+    most = pl.ds(0, DEVS - 1)
+    own.wait()
+    pltpu.make_async_copy(send.at[most], recv.at[most], recv_sem).wait()
 
     def part_copy(src, c, dst, to):
         rows = pl.ds(c * CHUNK, CHUNK)
@@ -204,36 +287,8 @@
         for dst, to in ((1, back), (3, flip_y), (4, flip_z)):
             part_copy(0, c, dst, to).start()
 
-    ready(0)
-    own_meta.wait()
-    pltpu.make_async_copy(small_send.at[0, most], small_got.at[most], meta_sems.at[1]).wait()
-    pltpu.make_async_copy(bc_here, bc_got, bc_sem.at[1]).wait()
-
-    @pl.when(listed != me)
-    def _():
-        pltpu.make_async_copy(bc_here, bc_got, bc_sem.at[0]).wait()
-
-    got = small_got[...].reshape(DEVS, 128)
-    turn = jnp.where(iota((128, ROWS), 1) % PAIR == iota((128, ROWS), 0), 1.0, 0.0)
-    at_row = jnp.dot(got, turn, precision=HIGH, preferred_element_type=F32)
-    at_row = jnp.where(iota((DEVS, ROWS), 1) // PAIR == iota((DEVS, ROWS), 0), at_row, 0.0)
-    own_pos = jnp.sum(at_row, axis=0, keepdims=True)
-    pos_row[...] = jnp.broadcast_to(own_pos, (8, ROWS))
-    block = own_pos.astype(jnp.int32) // BLK
-    own_cl = jnp.zeros((1, ROWS), F32)
-    for b in range(ROWS // BLK):
-        own_cl = own_cl + jnp.where(block == b, bc_got[b : b + 1, 0:1], 0.0)
-    clr[0] = jnp.broadcast_to(own_cl, (8, ROWS))
-    for dst, to in ((1, back), (2, back2), (3, flip_y), (4, flip_z), (5, flip_yz)):
-        pltpu.make_async_remote_copy(
-            clr.at[0], clr.at[dst], cl_send.at[dst], cl_recv.at[dst], device_id=place(to), device_id_type=MESH
-        ).start()
-    for c in range(1, CHUNKS):
+    for c in range(CHUNKS):
         ready(c)
-    clc[0] = column(own_cl)
-    posc[...] = column(pos_row[0:1])
-    for m in range(SLOTS):
-        acc[m] = jnp.full((8, ROWS), -1.0, F32)
 
     def fold(s, mask, hi, cols):
         kept = jnp.where(mask, s, -1.0)
@@ -250,10 +305,6 @@
             if diag:
                 mask = mask & (posc[rows, :] < pos_row[0:1, at])
             fold(s[:, k * 128 : (k + 1) * 128], mask, hi, at)
-
-    def cl_arrived(slot):
-        pltpu.make_async_copy(clr.at[slot], clr.at[slot], cl_recv.at[slot]).wait()
-        clc[slot] = column(clr[slot, 0:1])
 
     low = x < 2
 
@@ -280,11 +331,11 @@
         block_pair(0, 0, ROWS, 0, i * 512, 512, diag=True)
 
     forward(1)
-    for slot in (1, 3, 4):
-        cl_arrived(slot)
+    for slot in range(1, SLOTS):
+        pltpu.make_async_copy(clr.at[slot], clr.at[slot], cl_recv.at[slot]).wait()
+        clc[slot] = column(clr[slot, 0:1])
+
     forward(2)
-    for slot in (5, 2):
-        cl_arrived(slot)
     forward(3)
 
     ahead_hi = (x + step) % 4 > x
@@ -347,27 +398,38 @@
         best = jnp.maximum(best, acc_got[m - 1])
     best = jnp.max(best, axis=0, keepdims=True)
 
-    spread = jnp.where(iota((DEVS, ROWS), 1) // PAIR == iota((DEVS, ROWS), 0), best, 0.0)
-    fold8 = jnp.where(iota((ROWS, 128), 0) % PAIR == iota((ROWS, 128), 1), 1.0, 0.0)
-    ret = jnp.dot(spread, fold8, precision=HIGH, preferred_element_type=F32)
-    small_send[1] = ret.reshape(DEVS, 1, 128)
-    back_own = pltpu.make_async_copy(small_send.at[1, me], ret_got.at[me], local_sem.at[0])
-    back_own.start()
-
-    all_to_all(small_send.at[1], ret_got, me, core, y, z, x, ret_sems.at[0], ret_sems.at[1])
-    back_own.wait()
-    pltpu.make_async_copy(small_send.at[1, most], ret_got.at[most], ret_sems.at[1]).wait()
+    each = column(best).reshape(DEVS, PAIR, 128)
+    each = jnp.where(iota((DEVS, PAIR, 128), 1) == iota((DEVS, PAIR, 128), 2), each, 0.0)
+    ret_send[...] = jnp.sum(each, axis=1, keepdims=True)
+    stay = pltpu.make_async_copy(ret_send.at[dev], ret_got.at[dev], ret_local)
+    stay.start()
+    for k in range(1, DEVS):
+        j = k * 37 % DEVS
+        o, t = (owner + j // 16) % 8, (tile + j % 16) % 16
+        pltpu.make_async_remote_copy(
+            ret_send.at[o * 16 + t],
+            ret_got.at[dev],
+            ret_sems.at[0],
+            ret_sems.at[1],
+            device_id=(o, t),
+            device_id_type=MESH,
+        ).start()
+    stay.wait()
+    pltpu.make_async_copy(ret_send.at[most], ret_got.at[most], ret_sems.at[1]).wait()
     got = ret_got[...].reshape(DEVS, 128)
-    rank = rank_ref[...]
-    turn = jnp.where(rank % PAIR == iota((128, ROWS), 0), 1.0, 0.0)
-    rows = jnp.dot(got, turn, precision=HIGH, preferred_element_type=F32)
-    out_ref[...] = jnp.sum(
-        jnp.where(rank // PAIR == iota((DEVS, ROWS), 0), rows, 0.0), axis=0, keepdims=True
-    )
+    one = got.astype(BF16)
+    rest = got - one.astype(F32)
+    two = rest.astype(BF16)
+    three = (rest - two.astype(F32)).astype(BF16)
+    turn = turn_ref[...]
+    rows = jnp.dot(one, turn, preferred_element_type=F32)
+    rows = rows + jnp.dot(two, turn, preferred_element_type=F32)
+    rows = rows + jnp.dot(three, turn, preferred_element_type=F32)
+    out_ref[...] = jnp.sum(rows * mine_ref[...], axis=0, keepdims=True)
 
     pltpu.make_async_copy(send.at[most], recv.at[most], send_sem).wait()
-    pltpu.make_async_copy(small_send.at[0, most], small_got.at[most], meta_sems.at[0]).wait()
-    pltpu.make_async_copy(small_send.at[1, most], ret_got.at[most], ret_sems.at[0]).wait()
+    meta_left()
+    pltpu.make_async_copy(ret_send.at[most], ret_got.at[most], ret_sems.at[0]).wait()
     for c in range(CHUNKS):
         rows = pl.ds(c * CHUNK, CHUNK)
         for dst in (1, 3, 4, 5):
@@ -403,10 +465,14 @@
             pltpu.VMEM((SLOTS, ROWS, 128), F32),
             pltpu.VMEM((SLOTS, 8, ROWS), F32),
             pltpu.VMEM((SLOTS - 1, 8, ROWS), F32),
-            pltpu.VMEM((2, DEVS, 1, 128), F32),
+            pltpu.VMEM((8, 16, 1, 128), F32),
+            pltpu.VMEM((8, 16, 1, 128), F32),
+            pltpu.VMEM((16, 8, 1, 128), F32),
             pltpu.VMEM((DEVS, 1, 128), F32),
             pltpu.VMEM((DEVS, 1, 128), F32),
             pltpu.VMEM((1, ROWS), jnp.int32),
+            pltpu.VMEM((128, ROWS), BF16),
+            pltpu.VMEM((DEVS, ROWS), F32),
             pltpu.SemaphoreType.DMA,
             pltpu.SemaphoreType.DMA,
             pltpu.SemaphoreType.DMA((2,)),
@@ -417,8 +483,9 @@
             pltpu.SemaphoreType.DMA((SLOTS,)),
             pltpu.SemaphoreType.DMA((SLOTS,)),
             pltpu.SemaphoreType.DMA((2,)),
-            pltpu.SemaphoreType.DMA((2,)),
-            pltpu.SemaphoreType.REGULAR,
+            pltpu.SemaphoreType.DMA((4,)),
+            pltpu.SemaphoreType.DMA,
+            pltpu.SemaphoreType.DMA,
             pltpu.SemaphoreType.DMA((2,)),
         ],
         compiler_params=pltpu.CompilerParams(

time: 105 us -> 103 us (0.981)
  Pallas kernels: 104 us -> 102 us
    pallas_call x1, Pallas kernels: 104 us -> 102 us  [per_device(): pl.pallas_call(kernel, out_shape=jax.ShapeDtypeStruct((1, ROWS), F32), in...]
where the time goes in v3:
time: 103 us
  Pallas kernels  102 us (99%)
  local copies, waits for them, and re-layouts  1.28 us (1%)
    pallas_call x1, Pallas kernels, per_device(): pl.pallas_call(kernel, out_shape=jax.ShapeDtypeStruct((1, ROWS), F32), in...  102 us

profile of v3, /device:TPU:1, one launch (start us, length us, event | category | flops | bytes accessed | tf_op | source)
XLA Modules:
  0.0 102.9 jit_solution(10964412465658872297)
XLA Ops:
  0.0 101.6 %shard_map.37 = f32[1,1024]{1,0:T(1,128)} custom-call(bf16[1024,1024]{1,0:T(8,128)(2,1)} %x_ref.1, s32[1,1024]{1,0:T(1,128)} %bitcast.3, s32[8]{0:T(128)} %bc_ref.1), custom_call_target="tpu_custom_call" | custom-call | tf_op jit(solution)/shard_map/pallas_call | solution.py:450
  101.7 1.3 %copy.5 = f32[1024]{0:T(1024)} copy(f32[1024]{0:T(1024)} %bitcast.2) | data formatting | bytes 8192

commit v4 on v3

--- a/solution.py
+++ b/solution.py
@@ -89,10 +89,11 @@
 
 
 def kernel(
-    x_ref,
+    x_hbm,
     pos_ref,
     bc_ref,
     out_ref,
+    x_ref,
     unit,
     posc,
     send,
@@ -114,7 +115,7 @@
     turn_ref,
     mine_ref,
     send_sem,
-    recv_sem,
+    rows_sem,
     bc_sem,
     copy_send,
     copy_recv,
@@ -124,7 +125,7 @@
     acc_recv,
     ret_sems,
     meta_sems,
-    local_sem,
+    keep_sem,
     ret_local,
     meta_local,
 ):
@@ -135,6 +136,8 @@
     q = me % 4
     base = me - me % 16
     barrier = pltpu.get_barrier_semaphore()
+    x_in = pltpu.make_async_copy(x_hbm, x_ref, ret_local)
+    x_in.start()
 
     for k in range(1, DEVS):
         to = ((owner + k // 16) % 8, (tile + k % 16) % 16)
@@ -151,6 +154,8 @@
     within = jnp.concatenate(ranks, axis=1) & (PAIR - 1)
     to_o, to_t = place(pos >> 10)
     rank_ref[...] = (to_o * 16 + to_t) * PAIR + within
+
+    x_in.wait()
 
     @pl.loop(0, ROWS // 128)
     def _(c):
@@ -196,33 +201,49 @@
     def _():
         pltpu.make_async_copy(bc_here, bc_got, bc_sem.at[1]).start()
 
+    step = jnp.where(core == 0, 1, 3)
+
+    def send_rows(r, block, first):
+        @pl.loop(first, 32)
+        def _(k):
+            j = k * 13 % 32
+            o, zz = (owner + j // 4) % 8, (z + j) % 4
+            column_of = (x + r * (4 - (1 + 2 * (o % 2)))) % 4
+            to_x = column_of if r == 1 else x
+            pltpu.make_async_remote_copy(
+                send.at[o * 16 + zz * 4 + column_of],
+                recv.at[block, owner * 4 + z],
+                send_sem,
+                rows_sem.at[block],
+                device_id=(o, zz * 4 + to_x),
+                device_id_type=MESH,
+            ).start()
+
+    def keep_rows(r, block):
+        column_of = (x + r * (4 - step)) % 4
+        return pltpu.make_async_copy(
+            send.at[owner * 16 + z * 4 + column_of], recv.at[block, owner * 4 + z], keep_sem.at[block]
+        )
+
     meta_first, meta_second, meta_arrive, meta_left = rows_then_columns(
         meta_send, meta_mid, meta_got, owner, tile, meta_sems, meta_local
     )
     meta_first()
-
-    dev = owner * 16 + tile
-    own = pltpu.make_async_copy(send.at[dev], recv.at[dev], local_sem)
-    own.start()
-
-    def send_rows(first, last):
-        @pl.loop(first, last)
-        def _(k):
-            j = k * 37 % DEVS
-            o = (owner + j // 16) % 8
-            t = (tile // 4 + j // 4) % 4 * 4 + (tile + j) % 4
-            pltpu.make_async_remote_copy(
-                send.at[o * 16 + t],
-                recv.at[dev],
-                send_sem,
-                recv_sem,
-                device_id=(o, t),
-                device_id_type=MESH,
-            ).start()
-
-    send_rows(1, 48)
+    keep_rows(2, 3).start()
+    keep_rows(3, 2).start()
+    keep_rows(0, 0).start()
+    send_rows(2, 3, 1)
     meta_second()
-    send_rows(48, DEVS)
+    send_rows(3, 2, 1)
+    send_rows(0, 0, 1)
+    send_rows(1, 1, 0)
+
+    back = base + ((x + 4 - step) % 4) * 4 + q
+    back2 = base + ((x + 2) % 4) * 4 + q
+    ahead = base + ((x + step) % 4) * 4 + q
+    flip_y = me - q + (q + 2) % 4
+    flip_z = me - q + (q // 2) * 2 + (q + 1) % 2
+    flip_yz = me - q + 3 - q
 
     meta_arrive()
     pltpu.make_async_copy(bc_here, bc_got, bc_sem.at[1]).wait()
@@ -236,7 +257,9 @@
     turn = jnp.where(lane == (at & 7), 32.0, jnp.where(lane == (at & 7) + PAIR, 1.0, 0.0)).astype(BF16)
     at_row = jnp.dot(got, turn, preferred_element_type=F32)
     source = iota((DEVS, ROWS), 1) >> 3
-    at_row = jnp.where((source & 15) * 8 + (source >> 4) == iota((DEVS, ROWS), 0), at_row, 0.0)
+    source_x = (x + (source >> 5) * step) & 3
+    source = ((source & 3) * 4 + source_x) * 8 + ((source >> 2) & 7)
+    at_row = jnp.where(source == iota((DEVS, ROWS), 0), at_row, 0.0)
     own_pos = jnp.sum(at_row, axis=0, keepdims=True)
     pos_row[...] = jnp.broadcast_to(own_pos, (8, ROWS))
     block = own_pos.astype(jnp.int32) >> 7
@@ -244,14 +267,6 @@
     for b in range(ROWS // BLK):
         own_cl = own_cl + jnp.where(block == b, bc_got[b : b + 1, 0:1], 0.0)
     clr[0] = jnp.broadcast_to(own_cl, (8, ROWS))
-    step = jnp.where(core == 0, 1, 3)
-    back = base + ((x + 4 - step) % 4) * 4 + q
-    back2 = base + ((x + 2) % 4) * 4 + q
-    ahead = base + ((x + step) % 4) * 4 + q
-    flip_y = me - q + (q + 2) % 4
-    flip_z = me - q + (q // 2) * 2 + (q + 1) % 2
-    flip_yz = me - q + 3 - q
-
     for dst, to in ((1, back), (2, back2), (3, flip_y), (4, flip_z), (5, flip_yz)):
         pltpu.make_async_remote_copy(
             clr.at[0], clr.at[dst], cl_send.at[dst], cl_recv.at[dst], device_id=place(to), device_id_type=MESH
@@ -260,10 +275,6 @@
     posc[...] = column(own_pos)
     for m in range(SLOTS):
         acc[m] = jnp.full((8, ROWS), -1.0, F32)
-
-    most = pl.ds(0, DEVS - 1)
-    own.wait()
-    pltpu.make_async_copy(send.at[most], recv.at[most], recv_sem).wait()
 
     def part_copy(src, c, dst, to):
         rows = pl.ds(c * CHUNK, CHUNK)
@@ -280,15 +291,19 @@
         rows = pl.ds(c * CHUNK, CHUNK)
         pltpu.make_async_copy(parts.at[slot, rows], parts.at[slot, rows], copy_recv.at[slot, c]).wait()
 
-    def ready(c):
-        rows = pl.ds(c * CHUNK, CHUNK)
-        blocks = CHUNK // PAIR
-        parts[0, rows, :] = recv[pl.ds(c * blocks, blocks)].astype(F32).reshape(CHUNK, D).astype(BF16)
-        for dst, to in ((1, back), (3, flip_y), (4, flip_z)):
-            part_copy(0, c, dst, to).start()
-
-    for c in range(CHUNKS):
-        ready(c)
+    def rows_in(block, slot, r, remote):
+        most = pl.ds(0, remote)
+        pltpu.make_async_copy(recv.at[block, most], recv.at[block, most], rows_sem.at[block]).wait()
+        if remote < 32:
+            keep_rows(r, block).wait()
+        rows = pl.ds(r * CHUNK, CHUNK)
+        parts[slot, rows, :] = recv[block].astype(F32).reshape(CHUNK, D).astype(BF16)
+
+    rows_in(3, 2, 2, 31)
+    part_copy(2, 2, 1, ahead).start()
+    rows_in(2, 1, 3, 31)
+    part_copy(1, 3, 0, ahead).start()
+    part_copy(1, 3, 2, back).start()
 
     def fold(s, mask, hi, cols):
         kept = jnp.where(mask, s, -1.0)
@@ -308,82 +323,55 @@
 
     low = x < 2
 
-    def forward(c):
-        arrived(1, c)
-        if c < CHUNKS // 2:
-
-            @pl.when((x + 4 - step) % 4 < 2)
-            def _():
-                part_copy(1, c, 2, back).start()
-        else:
-            part_copy(1, c, 2, back).start()
-        arrived(3, c)
-        if c < CHUNKS // 2:
-            part_copy(3, c, 5, flip_z).start()
-        arrived(4, c)
-        if c >= CHUNKS // 2:
-            part_copy(4, c, 5, flip_y).start()
-
-    forward(0)
-
-    @pl.loop(0, 2)
-    def _(i):
-        block_pair(0, 0, ROWS, 0, i * 512, 512, diag=True)
-
-    forward(1)
-    for slot in range(1, SLOTS):
-        pltpu.make_async_copy(clr.at[slot], clr.at[slot], cl_recv.at[slot]).wait()
-        clc[slot] = column(clr[slot, 0:1])
-
-    forward(2)
-    forward(3)
+    rows_in(0, 0, 0, 31)
+    for dst, to in ((1, back), (3, flip_y), (4, flip_z)):
+        part_copy(0, 0, dst, to).start()
+    rows_in(1, 0, 1, 32)
+    for dst, to in ((1, back), (3, flip_y), (4, flip_z)):
+        part_copy(0, 1, dst, to).start()
+
+    def to_square(r):
+        arrived(0, r)
+        part_copy(0, r, 3, flip_y).start()
+        part_copy(0, r, 4, flip_z).start()
+
+    def to_back(r):
+        arrived(1, r)
+
+        @pl.when((x + 4 - step) % 4 < 2)
+        def _():
+            part_copy(1, r, 2, back).start()
+
+    def to_corner(slot, r):
+        arrived(slot, r)
+        part_copy(slot, r, 5, flip_z if slot == 3 else flip_y).start()
 
     ahead_hi = (x + step) % 4 > x
-
-    def with_ahead(face):
-        lo = jnp.where(ahead_hi, face, 1)
-        hi = jnp.where(ahead_hi, 1, face)
-
-        @pl.loop(0, 2)
-        def _(i):
-            block_pair(lo, 0, ROWS, hi, i * 512, 512)
+    ahead_lo = jnp.logical_not(ahead_hi)
+    high = jnp.logical_not(low)
+    half = ROWS // 2
+
+    def halves(a, ha, b, hb, a_hi):
+        lo, hi = jnp.where(a_hi, b, a), jnp.where(a_hi, a, b)
+        at_lo, at_hi = jnp.where(a_hi, hb, ha), jnp.where(a_hi, ha, hb)
+        block_pair(lo, at_lo * half, half, hi, at_hi * half, half)
+
+    def half_and_all(a, ha, b, a_hi):
+        @pl.when(a_hi)
+        def _():
+            block_pair(b, 0, ROWS, a, ha * half, half)
+
+        @pl.when(jnp.logical_not(a_hi))
+        def _():
+            block_pair(a, ha * half, half, b, 0, ROWS)
 
     def with_own(slot, mine_lo):
         lo = jnp.where(mine_lo, 0, slot)
         hi = jnp.where(mine_lo, slot, 0)
-        block_pair(lo, jnp.where(mine_lo, 0, 512), 512, hi, 0, ROWS)
-
-    with_ahead(0)
-    with_ahead(3)
-    with_ahead(4)
-    with_own(3, flip_y > me)
-    with_own(4, flip_z > me)
-    for c in range(CHUNKS):
-        arrived(5, c)
-    with_ahead(5)
-    with_own(5, flip_yz > me)
-
-    for n in range(CHUNKS):
-        if n < CHUNKS // 2:
-
-            @pl.when(low)
-            def _():
-                arrived(2, n)
-
-        else:
-            arrived(2, n)
-
-        @pl.when(low)
-        def _():
-            for face in (0, 3, 4, 5):
-                block_pair(face, 0, 512, 2, n * CHUNK, CHUNK)
-
-    @pl.when(jnp.logical_not(low))
-    def _():
-        for face in (0, 3, 4, 5):
-            block_pair(2, 512, 512, face, 0, ROWS)
-
-    for dst, to in ((1, ahead), (2, back2), (3, flip_y), (4, flip_z), (5, flip_yz)):
+        block_pair(lo, jnp.where(mine_lo, 0, half), half, hi, 0, ROWS)
+
+    def send_maxima(dst):
+        to = (None, ahead, back2, flip_y, flip_z, flip_yz)[dst]
         pltpu.make_async_remote_copy(
             acc.at[dst],
             acc_got.at[dst - 1],
@@ -392,6 +380,75 @@
             device_id=place(to),
             device_id_type=MESH,
         ).start()
+
+    arrived(1, 2)
+    part_copy(1, 2, 0, ahead).start()
+    to_square(3)
+    for slot in range(1, SLOTS):
+        pltpu.make_async_copy(clr.at[slot], clr.at[slot], cl_recv.at[slot]).wait()
+        clc[slot] = column(clr[slot, 0:1])
+    to_corner(3, 0)
+    to_corner(4, 1)
+    to_square(2)
+
+    @pl.loop(0, 2)
+    def _(i):
+        block_pair(0, 0, ROWS, 0, i * 512, 512, diag=True)
+
+    half_and_all(1, 1, 0, ahead_hi)
+    to_back(0)
+    arrived(3, 1)
+    arrived(4, 0)
+    halves(1, 1, 3, 0, ahead_hi)
+    halves(1, 1, 4, 0, ahead_hi)
+    to_back(1)
+    to_corner(3, 3)
+    arrived(2, 3)
+    for face in (0, 3, 4):
+        halves(2, 1, face, 0, low)
+    half_and_all(1, 0, 0, ahead_hi)
+    halves(1, 0, 3, 0, ahead_hi)
+    halves(1, 0, 4, 0, ahead_hi)
+    to_corner(4, 2)
+    arrived(3, 2)
+    arrived(4, 3)
+    half_and_all(3, 1, 1, ahead_lo)
+    half_and_all(4, 1, 1, ahead_lo)
+    with_own(3, flip_y > me)
+    with_own(4, flip_z > me)
+
+    @pl.when(high)
+    def _():
+        for face in (0, 3, 4):
+            block_pair(2, half, half, face, half, half)
+
+    arrived(5, 0)
+    arrived(5, 1)
+    half_and_all(5, 0, 1, ahead_lo)
+    halves(2, 1, 5, 0, low)
+
+    @pl.when(low)
+    def _():
+        arrived(2, 0)
+        arrived(2, 1)
+        for face in (0, 3, 4, 5):
+            block_pair(face, 0, half, 2, 0, half)
+
+    send_maxima(2)
+    send_maxima(3)
+    send_maxima(4)
+    arrived(5, 3)
+    arrived(5, 2)
+    half_and_all(5, 1, 1, ahead_lo)
+    with_own(5, flip_yz > me)
+
+    @pl.when(high)
+    def _():
+        block_pair(2, half, half, 5, half, half)
+
+    send_maxima(1)
+    send_maxima(5)
+
     best = acc[0]
     for m in range(1, SLOTS):
         pltpu.make_async_copy(acc_got.at[m - 1], acc_got.at[m - 1], acc_recv.at[m]).wait()
@@ -401,13 +458,16 @@
     each = column(best).reshape(DEVS, PAIR, 128)
     each = jnp.where(iota((DEVS, PAIR, 128), 1) == iota((DEVS, PAIR, 128), 2), each, 0.0)
     ret_send[...] = jnp.sum(each, axis=1, keepdims=True)
-    stay = pltpu.make_async_copy(ret_send.at[dev], ret_got.at[dev], ret_local)
+    dev = owner * 16 + tile
+    most = pl.ds(0, DEVS - 1)
+    stay = pltpu.make_async_copy(ret_send.at[owner * 4 + z], ret_got.at[dev], ret_local)
     stay.start()
     for k in range(1, DEVS):
         j = k * 37 % DEVS
-        o, t = (owner + j // 16) % 8, (tile + j % 16) % 16
+        o, zz = (owner + j // 4 % 8) % 8, (z + j % 4) % 4
+        t = zz * 4 + (x + j // 32 * step) % 4
         pltpu.make_async_remote_copy(
-            ret_send.at[o * 16 + t],
+            ret_send.at[j // 32 * 32 + o * 4 + zz],
             ret_got.at[dev],
             ret_sems.at[0],
             ret_sems.at[1],
@@ -427,18 +487,20 @@
     rows = rows + jnp.dot(three, turn, preferred_element_type=F32)
     out_ref[...] = jnp.sum(rows * mine_ref[...], axis=0, keepdims=True)
 
-    pltpu.make_async_copy(send.at[most], recv.at[most], send_sem).wait()
+    left = pl.ds(0, DEVS - 3)
+    pltpu.make_async_copy(send.at[left], send.at[left], send_sem).wait()
     meta_left()
     pltpu.make_async_copy(ret_send.at[most], ret_got.at[most], ret_sems.at[0]).wait()
     for c in range(CHUNKS):
         rows = pl.ds(c * CHUNK, CHUNK)
-        for dst in (1, 3, 4, 5):
-            pltpu.make_async_copy(parts.at[0, rows], parts.at[dst, rows], copy_send.at[dst, c]).wait()
-
-        @pl.when(((x + 4 - step) % 4 < 2) | (c >= CHUNKS // 2))
-        def _():
-            pltpu.make_async_copy(parts.at[1, rows], parts.at[2, rows], copy_send.at[2, c]).wait()
-
+        for dst in range(SLOTS):
+            if (dst, c) in ((0, 0), (0, 1), (1, 3), (2, 2)):
+                continue
+            sent = pltpu.make_async_copy(parts.at[0, rows], parts.at[dst, rows], copy_send.at[dst, c])
+            if (dst, c) in ((2, 0), (2, 1)):
+                pl.when((x + 4 - step) % 4 < 2)(sent.wait)
+            else:
+                sent.wait()
     for dst in range(1, SLOTS):
         pltpu.make_async_copy(clr.at[0], clr.at[dst], cl_send.at[dst]).wait()
         pltpu.make_async_copy(acc.at[dst], acc_got.at[dst - 1], acc_send.at[dst]).wait()
@@ -450,13 +512,14 @@
     out = pl.pallas_call(
         kernel,
         out_shape=jax.ShapeDtypeStruct((1, ROWS), F32),
-        in_specs=[vmem, vmem, pl.BlockSpec(memory_space=pltpu.SMEM)],
+        in_specs=[pl.BlockSpec(memory_space=pl.ANY), vmem, pl.BlockSpec(memory_space=pltpu.SMEM)],
         out_specs=vmem,
         scratch_shapes=[
             pltpu.VMEM((ROWS, D), BF16),
+            pltpu.VMEM((ROWS, D), BF16),
             pltpu.VMEM((ROWS, 128), F32),
             pltpu.VMEM((DEVS, PAIR, D), BF16),
-            pltpu.VMEM((DEVS, PAIR, D), BF16),
+            pltpu.VMEM((4, DEVS // 4, PAIR, D), BF16),
             pltpu.VMEM((SLOTS, ROWS, D), BF16),
             pltpu.VMEM((8, 128), F32),
             pltpu.VMEM((8, 128), F32),
@@ -474,7 +537,7 @@
             pltpu.VMEM((128, ROWS), BF16),
             pltpu.VMEM((DEVS, ROWS), F32),
             pltpu.SemaphoreType.DMA,
-            pltpu.SemaphoreType.DMA,
+            pltpu.SemaphoreType.DMA((4,)),
             pltpu.SemaphoreType.DMA((2,)),
             pltpu.SemaphoreType.DMA((SLOTS, CHUNKS)),
             pltpu.SemaphoreType.DMA((SLOTS, CHUNKS)),
@@ -484,7 +547,7 @@
             pltpu.SemaphoreType.DMA((SLOTS,)),
             pltpu.SemaphoreType.DMA((2,)),
             pltpu.SemaphoreType.DMA((4,)),
-            pltpu.SemaphoreType.DMA,
+            pltpu.SemaphoreType.DMA((4,)),
             pltpu.SemaphoreType.DMA,
             pltpu.SemaphoreType.DMA((2,)),
         ],

time: 103 us -> 98.6 us (0.957)
  Pallas kernels: 102 us -> 97.2 us
    pallas_call x1, Pallas kernels: 102 us -> 97.2 us  [per_device(): pl.pallas_call(kernel, out_shape=jax.ShapeDtypeStruct((1, ROWS), F32), in...]
where the time goes in v4:
time: 98.6 us; the launch traced here: 98.5 us
  Pallas kernels  97.2 us (99%)
  local copies, waits for them, and re-layouts  1.28 us (1%)
    pallas_call x1, Pallas kernels, per_device(): pl.pallas_call(kernel, out_shape=jax.ShapeDtypeStruct((1, ROWS), F32), in...  97.2 us

profile of v4, /device:TPU:1, one launch (start us, length us, event | category | flops | bytes accessed | tf_op | source)
XLA Modules:
  0.0 98.5 jit_solution(11365397200266481294)
XLA Ops:
  0.0 97.2 %shard_map.37 = f32[1,1024]{1,0:T(1,128)} custom-call(bf16[1024,1024]{1,0:T(8,128)(2,1)} %x_hbm.1, s32[1,1024]{1,0:T(1,128)} %bitcast.3, s32[8]{0:T(128)} %bc_ref.1), custom_call_target="tpu_custom_call" | custom-call | tf_op jit(solution)/shard_map/pallas_call | solution.py:512
  97.2 1.3 %copy.5 = f32[1024]{0:T(1024)} copy(f32[1024]{0:T(1024)} %bitcast.2) | data formatting | bytes 8192

commit v5 on v4

--- a/solution.py
+++ b/solution.py
@@ -17,6 +17,13 @@
 BF16 = jnp.bfloat16
 MESH = pl.DeviceIdType.MESH
 NT = (((1,), (1,)), ((), ()))
+
+
+def distance(j):
+    return 2 * min(j // 32, 4 - j // 32) + min(j // 4 % 8, 8 - j // 4 % 8) + 2 * min(j % 4, 4 - j % 4)
+
+
+FAR_FIRST = sorted(range(1, DEVS), key=lambda j: (-distance(j), j * 37 % DEVS))
 
 
 def place(part):
@@ -388,14 +395,17 @@
         pltpu.make_async_copy(clr.at[slot], clr.at[slot], cl_recv.at[slot]).wait()
         clc[slot] = column(clr[slot, 0:1])
     to_corner(3, 0)
+    halves(1, 1, 0, 0, ahead_hi)
     to_corner(4, 1)
+    arrived(2, 3)
+    halves(2, 1, 0, 0, low)
     to_square(2)
 
     @pl.loop(0, 2)
     def _(i):
         block_pair(0, 0, ROWS, 0, i * 512, 512, diag=True)
 
-    half_and_all(1, 1, 0, ahead_hi)
+    halves(1, 1, 0, 1, ahead_hi)
     to_back(0)
     arrived(3, 1)
     arrived(4, 0)
@@ -403,8 +413,7 @@
     halves(1, 1, 4, 0, ahead_hi)
     to_back(1)
     to_corner(3, 3)
-    arrived(2, 3)
-    for face in (0, 3, 4):
+    for face in (3, 4):
         halves(2, 1, face, 0, low)
     half_and_all(1, 0, 0, ahead_hi)
     halves(1, 0, 3, 0, ahead_hi)
@@ -440,13 +449,13 @@
     arrived(5, 3)
     arrived(5, 2)
     half_and_all(5, 1, 1, ahead_lo)
+    send_maxima(1)
     with_own(5, flip_yz > me)
 
     @pl.when(high)
     def _():
         block_pair(2, half, half, 5, half, half)
 
-    send_maxima(1)
     send_maxima(5)
 
     best = acc[0]
@@ -462,8 +471,7 @@
     most = pl.ds(0, DEVS - 1)
     stay = pltpu.make_async_copy(ret_send.at[owner * 4 + z], ret_got.at[dev], ret_local)
     stay.start()
-    for k in range(1, DEVS):
-        j = k * 37 % DEVS
+    for j in FAR_FIRST:
         o, zz = (owner + j // 4 % 8) % 8, (z + j % 4) % 4
         t = zz * 4 + (x + j // 32 * step) % 4
         pltpu.make_async_remote_copy(

time: 98.6 us -> 97.3 us (0.987)
  Pallas kernels: 97.2 us -> 95.8 us
    pallas_call x1, Pallas kernels: 97.2 us -> 95.8 us  [per_device(): pl.pallas_call(kernel, out_shape=jax.ShapeDtypeStruct((1, ROWS), F32), in...]
where the time goes in v5:
time: 97.3 us; the launch traced here: 97.1 us
  Pallas kernels  95.8 us (98%)
  local copies, waits for them, and re-layouts  1.28 us (1%)
    pallas_call x1, Pallas kernels, per_device(): pl.pallas_call(kernel, out_shape=jax.ShapeDtypeStruct((1, ROWS), F32), in...  95.8 us

profile of v5, /device:TPU:1, one launch (start us, length us, event | category | flops | bytes accessed | tf_op | source)
XLA Modules:
  0.0 97.1 jit_solution(15752739367500472744)
XLA Ops:
  0.0 95.8 %shard_map.37 = f32[1,1024]{1,0:T(1,128)} custom-call(bf16[1024,1024]{1,0:T(8,128)(2,1)} %x_hbm.1, s32[1,1024]{1,0:T(1,128)} %bitcast.3, s32[8]{0:T(128)} %bc_ref.1), custom_call_target="tpu_custom_call" | custom-call | tf_op jit(solution)/shard_map/pallas_call | solution.py:520
  95.9 1.3 %copy.5 = f32[1024]{0:T(1024)} copy(f32[1024]{0:T(1024)} %bitcast.2) | data formatting | bytes 8192

commit v6 on v5

--- a/solution.py
+++ b/solution.py
@@ -213,7 +213,7 @@
     def send_rows(r, block, first):
         @pl.loop(first, 32)
         def _(k):
-            j = k * 13 % 32
+            j = k * 11 % 32
             o, zz = (owner + j // 4) % 8, (z + j) % 4
             column_of = (x + r * (4 - (1 + 2 * (o % 2)))) % 4
             to_x = column_of if r == 1 else x
@@ -388,18 +388,22 @@
             device_id_type=MESH,
         ).start()
 
+    def clusters_in(*slots):
+        for slot in slots:
+            pltpu.make_async_copy(clr.at[slot], clr.at[slot], cl_recv.at[slot]).wait()
+            clc[slot] = column(clr[slot, 0:1])
+
     arrived(1, 2)
     part_copy(1, 2, 0, ahead).start()
     to_square(3)
-    for slot in range(1, SLOTS):
-        pltpu.make_async_copy(clr.at[slot], clr.at[slot], cl_recv.at[slot]).wait()
-        clc[slot] = column(clr[slot, 0:1])
+    clusters_in(1, 2)
     to_corner(3, 0)
     halves(1, 1, 0, 0, ahead_hi)
     to_corner(4, 1)
     arrived(2, 3)
     halves(2, 1, 0, 0, low)
     to_square(2)
+    clusters_in(3, 4, 5)
 
     @pl.loop(0, 2)
     def _(i):

time: 97.3 us -> 96.7 us (level)
  no operation moved by 1% of the time
where the time goes in v6:
time: 96.7 us; the launch traced here: 96.5 us
  Pallas kernels  95.2 us (98%)
  local copies, waits for them, and re-layouts  1.28 us (1%)
    pallas_call x1, Pallas kernels, per_device(): pl.pallas_call(kernel, out_shape=jax.ShapeDtypeStruct((1, ROWS), F32), in...  95.2 us

profile of v6, /device:TPU:1, one launch (start us, length us, event | category | flops | bytes accessed | tf_op | source)
XLA Modules:
  0.0 96.5 jit_solution(7896166268252760110)
XLA Ops:
  0.0 95.2 %shard_map.37 = f32[1,1024]{1,0:T(1,128)} custom-call(bf16[1024,1024]{1,0:T(8,128)(2,1)} %x_hbm.1, s32[1,1024]{1,0:T(1,128)} %bitcast.3, s32[8]{0:T(128)} %bc_ref.1), custom_call_target="tpu_custom_call" | custom-call | tf_op jit(solution)/shard_map/pallas_call | solution.py:524
  95.3 1.3 %copy.5 = f32[1024]{0:T(1024)} copy(f32[1024]{0:T(1024)} %bitcast.2) | data formatting | bytes 8192
